TPU v7x, 256 devices: a whole 4x4x8 slice. The times are simulated.
256 devices in a mesh: dom: 64 (over y, z, core), sub: 4 (over x).
Axes of the slice: x: 4, y: 4, z: 8, core: 2. Of those that a mesh axis runs over, the one named last changes fastest.
Arguments:
- dofs: float32 [35, 9, 32768], P(None, None, ('dom', 'sub')), may hold values from -6 to 6
- stiffness: float32 [3, 35, 35], replicated
- star: float32 [3, 9, 9, 32768], P(None, None, None, ('dom', 'sub'))
- local_flux: float32 [4, 9, 9, 32768], P(None, None, None, ('dom', 'sub'))
- neighbour_flux: float32 [4, 9, 9, 32768], P(None, None, None, ('dom', 'sub'))
- face_proj: float32 [4, 15, 35], replicated, may hold values from -1 to 1
- face_rot: float32 [3, 15, 15], replicated
- cluster: int32 [32768], P(('dom', 'sub')), may hold values from 0 to 3, as said below
- neighbour: int32 [4, 32768], P(None, ('dom', 'sub')), may hold values from 0 to 896, as said below
- orient: int32 [4, 32768], P(None, ('dom', 'sub')), may hold values from 0 to 2
- send_list: int32 [64, 4, 96], P('dom', 'sub'), may hold values from 0 to 512, as said below
Outputs:
- dofs_out: float32 [35, 9, 32768], P(None, None, ('dom', 'sub'))
Inputs may be any that keep to these rules, and one draw needn't show every extreme that they name: Along a device's 128 elements the cluster ids never fall. On every device clusters 0, 1 and 2 hold at most 32 elements each, and for each of the three some device holds exactly that many. `send_list`: entry (b * 4 + t) * 8 + l of a device's list names the face j * 128 + n (face j of its element n) whose data go to the device b - 1 steps further along dom at sub index t, in slot l of that link; 512 marks an empty slot. The live slots of a link come first, both ends of a link use the same number of slots, and some link fills all 8. No slot leads past an end of dom or to the device itself. For face i of element n on a device: a code c below 512 names face c // 128 of element c % 128 on the same device; a code 4 * 128 + 4 k + f names face f of the element held by slot k of the data that reach the device, where k = (b * 4 + t) * 8 + l is slot l of the link from the device at sub index t that lies b - 1 steps lower along dom; 896 marks a boundary face. Faces neighbour each other in pairs.
All inputs are finite; a program needn't handle non-finite values.
Results may differ from a plain program's by a relative error of at most 0.0001.
Values sent between devices are 32-bit elements; how exact they have to be, the bound alone decides.
No kernel may reach another device: no remote copies, remote signals or barrier semaphores. Data moves between devices by JAX's collectives and lax.ppermute only.
A program may use at most 192 MiB of HBM per device.

v0:
```python
import functools

import jax
import jax.numpy as jnp
from jax import lax
from jax.experimental import pallas as pl
from jax.experimental.pallas import tpu as pltpu
from jax.sharding import PartitionSpec as P

ORDER = 5
STEPS = 8
NB = 35
NBP = 40
NBK = 48
NF = 15
NFP = 16
NV = 9
E = 128
H = 8
SLOTS = 96
FACES = 4 * E
WIDE = NV * NFP
COLS = NV * E
FACT = [1.0, 1.0, 2.0, 6.0, 24.0, 120.0, 720.0]
BF = jnp.bfloat16
F32 = jnp.float32


def halves(x):
    hi = x.astype(BF)
    lo = (x - hi.astype(F32)).astype(BF)
    return hi, lo


def dot(a, b):
    return jnp.dot(a, b, preferred_element_type=F32)


def fill_basis(xs_ref, values):
    pad = jnp.zeros((NBK - NBP, E), F32)
    for v in range(len(values)):
        hi, lo = halves(jnp.concatenate([values[v], pad], axis=0))
        cols = slice(v * E, (v + 1) * E)
        xs_ref[0:NBK, cols] = hi
        xs_ref[NBK : 2 * NBK, cols] = lo
        xs_ref[2 * NBK : 3 * NBK, cols] = hi


def derive(values, stiff_ref, star_ref, xs_ref):
    fill_basis(xs_ref, values)
    stiff = stiff_ref[...]
    chunks = [range(0, 4), range(4, 8), range(8, 9)]
    applied = [dot(stiff, xs_ref[:, c[0] * E : (c[-1] + 1) * E]) for c in chunks]
    acc = [None] * NV
    for chunk, piece in zip(chunks, applied):
        for d in range(3):
            for n, u in enumerate(chunk):
                part = piece[d * NBP : (d + 1) * NBP, n * E : (n + 1) * E]
                for v in range(NV):
                    term = part * star_ref[u, v, d : d + 1, :]
                    acc[v] = term if acc[v] is None else acc[v] + term
    return acc


def lane_group(shape):
    return lax.broadcasted_iota(jnp.int32, shape, len(shape) - 1) >> 5


def shifted(x, groups):
    return x if groups % 4 == 0 else pltpu.roll(x, groups % 4 * 32, x.ndim - 1)


def side_by_side(values):
    group = lane_group(values[0].shape)
    parts = []
    for j in range(3):
        part = jnp.zeros_like(values[0])
        for g in range(min(4, len(values) - 4 * j)):
            part = jnp.where(group == g, shifted(values[4 * j + g], g), part)
        parts.append(part)
    return parts


def apart(parts):
    return [shifted(parts[v // 4], -(v % 4)) for v in range(NV)]


def thin_matrices(full_ref, thin_ref):
    picks = []
    for to in range(2):
        for of in range(2):
            for r in range(4):
                picks.append([(4 * of + (g - r) % 4, 4 * to + g) for g in range(4)])
    picks += [[(8, g) for g in range(4)], [(8, 4 + g) for g in range(4)]]
    picks += [[(g, 8) for g in range(4)], [(4 + g, 8) for g in range(4)], [(8, 8)]]
    depth = full_ref.shape[2]
    group = lane_group((depth, E))
    for n, sources in enumerate(picks):
        row = jnp.zeros((depth, E), F32)
        for g, (u, v) in enumerate(sources):
            row = jnp.where(group == g, shifted(full_ref[u, v], g), row)
        thin_ref[n] = row


def mix(acc, parts, thin_ref, d):
    first, second, third = parts
    spread = third + shifted(third, 1)
    spread = spread + shifted(spread, 2)
    terms = [[], [], []]
    for r in range(4):
        one, two = shifted(first, r), shifted(second, r)
        for to in range(2):
            terms[to].append(one * thin_ref[8 * to + r, d : d + 1, :])
            terms[to].append(two * thin_ref[8 * to + 4 + r, d : d + 1, :])
    for to in range(2):
        terms[to].append(spread * thin_ref[16 + to, d : d + 1, :])
    terms[2] = [part * thin_ref[18 + n, d : d + 1, :] for n, part in enumerate(parts)]
    for to in range(3):
        for term in terms[to]:
            acc[to] = term if acc[to] is None else acc[to] + term


def mixed_parts(acc):
    last = acc[2] + shifted(acc[2], 2)
    last = last + shifted(last, 1)
    return [acc[0], acc[1], jnp.where(lane_group(last.shape) == 0, last, 0.0)]


def derive_thin(parts, stiff_ref, thin_ref, xt_ref):
    fill_basis(xt_ref, parts)
    applied = dot(stiff_ref[...], xt_ref[...])
    acc = [None] * 3
    for d in range(3):
        rows = applied[d * NBP : (d + 1) * NBP]
        mix(acc, [rows[:, j * E : (j + 1) * E] for j in range(3)], thin_ref, d)
    return mixed_parts(acc)


def weight_rows(cluster_ref, step):
    period = jnp.left_shift(jnp.int32(1), cluster_ref[...])
    offset = jnp.bitwise_and(jnp.int32(step), period - 1)
    a, inverse = offset.astype(F32), 1.0 / period.astype(F32)
    low, high, scale, rows = jnp.ones_like(a), jnp.ones_like(a), jnp.ones_like(a), []
    for k in range(ORDER):
        low, high = low * a, high * (a + 1.0)
        rows.append((high - low) * scale * (1.0 / FACT[k + 1]))
        scale = scale * inverse
    return rows, offset == 0


def expand_thin(step, upd, cluster, stiff, thin, proj, pick, terms_in, terms, d_hi, d_lo, pay_swap, pay_rest, xs, xt):
    rows, start = weight_rows(cluster, step)
    current = side_by_side(upd)
    fresh = [None] * 3
    for k in range(ORDER):
        if k > 0:
            current = derive_thin(current, stiff, thin, xt)
        for j in range(3):
            terms[k, j] = current[j]
            part = current[j] * (1.0 / FACT[k + 1])
            fresh[j] = part if k == 0 else fresh[j] + part
    fresh = apart(fresh)
    total = []
    for v in range(NV):
        kept = terms_in[0, v] * rows[0]
        for k in range(1, ORDER):
            kept = kept + terms_in[k, v] * rows[k]
        total.append(jnp.where(start, fresh[v], kept))
    send(total, proj, pick, d_hi, d_lo, pay_swap, pay_rest, xs)


def expand(step, first, upd, cluster, stiff, star, proj, pick, terms_in, terms, d_hi, d_lo, pay_swap, pay_rest, xs):
    rows, start = weight_rows(cluster, step)
    current = upd
    total = [None] * NV
    for k in range(ORDER):
        if k > 0:
            current = derive(current, stiff, star, xs)
        for v in range(NV):
            kept = current[v] if first else jnp.where(start, current[v], terms_in[k, v])
            terms[k, v] = kept
            part = kept * rows[k]
            total[v] = part if k == 0 else total[v] + part
    send(total, proj, pick, d_hi, d_lo, pay_swap, pay_rest, xs)


def send(total, proj, pick, d_hi, d_lo, pay_swap, pay_rest, xs):
    fill_basis(xs, total)
    faces = dot(proj[...], xs[...])
    for i in range(4):
        for v in range(NV):
            hi, lo = halves(faces[i * NFP : (i + 1) * NFP, v * E : (v + 1) * E])
            d_hi[v * NFP : (v + 1) * NFP, i * E : (i + 1) * E] = hi
            d_lo[v * NFP : (v + 1) * NFP, i * E : (i + 1) * E] = lo
    dims = (((1,), (1,)), ((), ()))
    pay = lax.dot_general(pick[...], d_hi[...], dims, preferred_element_type=F32)
    pay = pay + lax.dot_general(pick[...], d_lo[...], dims, preferred_element_type=F32)
    pay_swap[...] = pay[0:32]
    pay_rest[...] = pay[32:160]


def opening(*refs):
    raw, refs = refs[:11], list(refs[11:])
    take = lambda n: [refs.pop(0) for _ in range(n)]
    odd_ref = refs.pop(0)
    neighbour_ref, cluster, orient = take(3)
    stiff, proj, star, nflux, lflux, lift_a, lift_b, own_lift, far, pick = take(10)
    terms, d_hi, d_lo, pay_swap, pay_rest = take(5)
    dofs_s, stiff_s, proj_s, rot_s, send_ref, state, wide_s, tall_s, xs, sems = take(10)
    targets = [send_ref, neighbour_ref, stiff_s, proj_s, rot_s, cluster, dofs_s, star, nflux, lflux, orient]
    copies = [pltpu.make_async_copy(raw[n], targets[n], sems.at[n]) for n in range(11)]
    for copy in copies:
        copy.start()
    for copy in copies[:2]:
        copy.wait()

    high = lax.Precision.HIGHEST
    columns_first = (((0,), (0,)), ((), ()))

    def grid(shape):
        return lax.broadcasted_iota(jnp.int32, shape, 0), lax.broadcasted_iota(jnp.int32, shape, 1)

    odd = odd_ref[...]
    codes = neighbour_ref[...]
    slot = jnp.right_shift(codes - FACES, 2)
    block, source, place = slot >> 5, jnp.bitwise_and(slot >> 3, 3), jnp.bitwise_and(slot, 7)
    same, cross = 4 * (1 - odd), 4 * odd
    row = jnp.where(block == 2 * (1 - odd), (cross + source) * 16 + place, (same + source) * 16 + place)
    row = jnp.where(block == 2 * odd, row + H, row)
    row = jnp.where((codes >= FACES) & (codes < FACES + 4 * SLOTS), row, -1)
    rows, _ = grid((128, E))
    for i in range(4):
        far[:, i * E : (i + 1) * E] = (rows == row[i : i + 1, :]).astype(F32).astype(BF)
    rows, columns = grid((160, SLOTS))
    flag = odd[:, 0:1]
    rest = rows - 32
    peer, place = rest >> 4, jnp.bitwise_and(rest, 15)
    inside = jnp.where((peer >> 2) == 1 - flag, 32, 64 * flag)
    wanted = inside + jnp.bitwise_and(peer, 3) * H + place
    wanted = jnp.where(rest < 0, 64 * (1 - flag) + rows, jnp.where(place < H, wanted, -1))
    chooser = (columns == wanted).astype(F32)
    listed = jnp.broadcast_to(send_ref[...].astype(F32), (8, SLOTS))
    listed = lax.dot_general(chooser, listed, (((1,), (1,)), ((), ())), precision=high, preferred_element_type=F32)
    listed = jnp.where(wanted[:, 0:1] < 0, float(FACES), listed[:, 0:1])
    _, columns = grid((160, FACES))
    pick[...] = (columns.astype(F32) == listed).astype(F32).astype(BF)

    for copy in copies[2:5]:
        copy.wait()
    wide_s[...] = jnp.zeros_like(wide_s)
    for d in range(3):
        wide_s[d * NBP : d * NBP + NB, 0:NB] = -stiff_s[d]
    rows, columns = grid((NBK, 3 * NBK))
    twice = ((columns == rows) | (columns == rows + NBK)).astype(F32).astype(BF)
    once = (columns == rows + 2 * NBK).astype(F32).astype(BF)
    hi, lo = halves(wide_s[...])
    stiff[...] = (dot(hi, twice) + dot(lo, once)).astype(BF)
    tall_s[...] = jnp.zeros_like(tall_s)
    for i in range(4):
        for f in range(NF):
            tall_s[i * NFP + f : i * NFP + f + 1, 0:NB] = proj_s[f, i : i + 1, :]
    hi, lo = halves(tall_s[...])
    proj[...] = (dot(hi, twice) + dot(lo, once)).astype(BF)
    rows, columns = grid((64, 192))
    twice = ((columns == rows) | (columns == rows + 64)).astype(F32).astype(BF)
    once = (columns == rows + 128).astype(F32).astype(BF)
    own = lax.dot_general(hi, twice, columns_first, preferred_element_type=F32)
    own = own + lax.dot_general(lo, once, columns_first, preferred_element_type=F32)
    own_lift[...] = own[0:NBP].astype(BF)
    mixed = jnp.zeros((64, 192), F32)
    to_rows, to_columns = grid((64, NF))
    from_rows, from_columns = grid((NF, 192))
    for o in range(3):
        spread = (jnp.bitwise_and(to_rows, 15) == to_columns).astype(F32)
        spread = jnp.dot(spread, rot_s[o], precision=high, preferred_element_type=F32)
        group = from_columns // 48
        placed = (from_columns - 48 * group == o * NFP + from_rows).astype(F32)
        mixed = mixed + jnp.dot(spread, placed, precision=high, preferred_element_type=F32)
    mixed = jnp.where((rows >> 4) == columns // 48, mixed, 0.0)
    lift = lax.dot_general(tall_s[...], mixed, columns_first, precision=high, preferred_element_type=F32)
    hi, lo = halves(lift[0:NBP])
    lift_a[0:NBP, :] = hi
    lift_a[NBP : 2 * NBP, :] = lo
    lift_b[...] = hi

    for copy in copies[5:]:
        copy.wait()
    state[...] = jnp.zeros_like(state)
    for v in range(NV):
        state[v, 0:NB, :] = dofs_s[v]
    upd = [state[v] for v in range(NV)]
    expand(0, True, upd, cluster, stiff, star, proj, pick, None, terms, d_hi, d_lo, pay_swap, pay_rest, xs)


def critical(last, step, *refs):
    refs = list(refs)
    take = lambda n: [refs.pop(0) for _ in range(n)]
    got_ref, nsum_ref, base_ref, nflux, lift_a, lift_b, orient, far = take(8)
    if last:
        out_ref, xg = take(2)
    else:
        stiff, star, proj, pick, cluster, terms_in = take(6)
        nsum_out, terms, d_hi, d_lo, pay_swap, pay_rest, xg, xs = take(8)
        if step % 2:
            (xt,) = take(1)

    got_hi, got_lo = halves(got_ref[...])
    dims = (((0,), (0,)), ((), ()))
    arrived = lax.dot_general(got_hi, far[...], dims, preferred_element_type=F32)
    arrived = arrived + lax.dot_general(got_lo, far[...], dims, preferred_element_type=F32)
    total = nsum_ref[...] + arrived
    if not last:
        nsum_out[...] = total
    for i in range(4):
        acc = [None] * NV
        for u in range(NV):
            part = total[u * NFP : (u + 1) * NFP, i * E : (i + 1) * E]
            for v in range(NV):
                term = part * nflux[u, v, i : i + 1, :]
                acc[v] = term if acc[v] is None else acc[v] + term
        chosen = []
        for o in range(3):
            mask = (orient[i : i + 1, :] == o).astype(F32)
            chosen.append(jnp.broadcast_to(mask, (NFP, E)).astype(BF))
        for v in range(NV):
            hi, lo = halves(acc[v])
            for o in range(3):
                row = (i * 3 + o) * NFP
                cols = slice(v * E, (v + 1) * E)
                xg[row : row + NFP, cols] = hi * chosen[o]
                xg[192 + row : 192 + row + NFP, cols] = lo * chosen[o]
    two = dot(lift_a[...], xg[0:192, :])
    lifted = two[0:NBP] + two[NBP : 2 * NBP] + dot(lift_b[...], xg[192:384, :])
    upd = [base_ref[v] + lifted[:, v * E : (v + 1) * E] for v in range(NV)]
    if last:
        for v in range(NV):
            out_ref[v] = upd[v][0:NB]
    elif step % 2:
        expand_thin(
            step, upd, cluster, stiff, star, proj, pick, terms_in, terms, d_hi, d_lo, pay_swap, pay_rest, xs, xt
        )
    else:
        expand(step, False, upd, cluster, stiff, star, proj, pick, terms_in, terms, d_hi, d_lo, pay_swap, pay_rest, xs)


def beside(step, *refs):
    refs = list(refs)
    take = lambda n: [refs.pop(0) for _ in range(n)]
    first, thin = step == 0, step % 2 == 1
    terms, d_hi, d_lo, neighbour, stiff, star, proj, lflux, own_lift, cluster = take(10)
    if not first:
        nsum_ref, base_ref = take(2)
    nsum_out, base_out = take(2)
    if first:
        thin_star, thin_lflux = take(2)
    xs, xq = take(2)
    _, start = weight_rows(cluster, step)
    period = jnp.left_shift(jnp.int32(1), cluster[...]).astype(F32)
    face_rows = lax.broadcasted_iota(jnp.int32, (FACES, E), 0)
    for i in range(4):
        cols = slice(i * E, (i + 1) * E)
        near = (face_rows == neighbour[i : i + 1, :]).astype(F32).astype(BF)
        gathered = dot(d_hi[...], near) + dot(d_lo[...], near)
        nsum_out[:, cols] = gathered if first else gathered + jnp.where(start, 0.0, nsum_ref[:, cols])
    wide = 3 if thin else NV
    held = [[terms[k, v] for v in range(wide)] for k in range(ORDER)]
    if thin:
        final = derive_thin(held[ORDER - 1], stiff, star, xs)
    else:
        final = derive(held[ORDER - 1], stiff, star, xs)
    state = []
    whole = []
    for v in range(wide):
        volume = final[v] * (1.0 / FACT[ORDER])
        own = held[0][v]
        for k in range(1, ORDER):
            volume = volume + held[k][v] * (1.0 / FACT[k])
            own = own + held[k][v] * (1.0 / FACT[k + 1])
        state.append(held[0][v] + volume)
        whole.append(own if thin else own * period)
    fill_basis(xs, whole)
    faces = dot(proj[...], xs[...])
    for i in range(4):
        rows = faces[i * NFP : (i + 1) * NFP]
        acc = [None] * wide
        if thin:
            mix(acc, [rows[:, j * E : (j + 1) * E] for j in range(3)], lflux, i)
            acc = mixed_parts(acc)
        else:
            for u in range(NV):
                part = rows[:, u * E : (u + 1) * E]
                for v in range(NV):
                    term = part * lflux[u, v, i : i + 1, :]
                    acc[v] = term if acc[v] is None else acc[v] + term
        for v in range(wide):
            hi, lo = halves(acc[v])
            cols = slice(v * E, (v + 1) * E)
            xq[i * NFP : (i + 1) * NFP, cols] = hi
            xq[64 + i * NFP : 64 + (i + 1) * NFP, cols] = lo
            xq[128 + i * NFP : 128 + (i + 1) * NFP, cols] = hi
    lifted = dot(own_lift[...], xq[...])
    fresh = [state[v] - lifted[:, v * E : (v + 1) * E] for v in range(wide)]
    if thin:
        fresh = apart(fresh)
    for v in range(NV):
        base_out[v] = fresh[v] if first else jnp.where(start, fresh[v], base_ref[v])
    if first:
        thin_matrices(star, thin_star)
        thin_matrices(lflux, thin_lflux)


def call(kernel, outs, scratch, args, raw=0):
    def memory(s):
        return pltpu.VMEM(*s) if isinstance(s, tuple) else s

    return pl.pallas_call(
        kernel,
        out_shape=[jax.ShapeDtypeStruct(s, t) for s, t in outs],
        in_specs=[pl.BlockSpec(memory_space=pltpu.HBM if n < raw else pltpu.VMEM) for n in range(len(args))],
        out_specs=[pl.BlockSpec(memory_space=pltpu.VMEM)] * len(outs),
        scratch_shapes=[memory(s) for s in scratch],
        compiler_params=pltpu.CompilerParams(vmem_limit_bytes=40 * 1024 * 1024),
    )(*args)


def body(dofs, stiffness, star, local_flux, neighbour_flux, face_proj, face_rot, cluster, neighbour, orient, send_list):
    n_dom, n_sub = lax.axis_size("dom"), lax.axis_size("sub")
    odd = lax.axis_index("dom") % 2
    chip = [(i, i ^ 1) for i in range(n_dom)]
    groups = [
        [(i + h) % n_dom * n_sub + t for h in range(2) for t in range(n_sub)] for i in range(1, n_dom, 2)
    ]
    lines = [[i * n_sub + t for t in range(n_sub)] for i in range(n_dom)]
    dom = lax.axis_index("dom")
    at_end = (dom == 0) | (dom == n_dom - 1)

    def exchange(block, among):
        return lax.all_to_all(
            block, ("dom", "sub"), split_axis=0, concat_axis=0, tiled=True, axis_index_groups=among
        )

    def across_pair(block):
        return exchange(block, groups)

    def within_line(block):
        own = exchange(jnp.where(odd == 1, block[0:4], block[4:8]), lines)
        return jnp.concatenate([own, own])

    holds_swapped = (jnp.arange(8, dtype=jnp.int32) // 4 == 1 - odd)[:, None, None]
    raw = [
        send_list.reshape(1, SLOTS),
        neighbour,
        stiffness,
        jnp.transpose(face_proj, (1, 0, 2)),
        face_rot,
        cluster.reshape(1, E),
        jnp.transpose(dofs, (1, 0, 2)),
        jnp.transpose(star, (1, 2, 0, 3)),
        jnp.transpose(neighbour_flux, (1, 2, 0, 3)),
        jnp.transpose(local_flux, (1, 2, 0, 3)),
        orient,
    ]
    raw = [pltpu.with_memory_space_constraint(x, pltpu.HBM) for x in raw]
    flux_s = ((NV, NV, 4, E), F32)
    constants = [
        ((4, E), jnp.int32),
        ((1, E), jnp.int32),
        ((4, E), jnp.int32),
        ((3 * NBP, 3 * NBK), BF),
        ((4 * NFP, 3 * NBK), BF),
        ((NV, NV, 3, E), F32),
        flux_s,
        flux_s,
        ((2 * NBP, 192), BF),
        ((NBP, 192), BF),
        ((NBP, 192), BF),
        ((128, FACES), BF),
        ((160, FACES), BF),
    ]
    terms_s = ((ORDER, NV, NBP, E), F32)
    face_s = ((WIDE, FACES), BF)
    nsum_s = ((WIDE, FACES), F32)
    base_s = ((NV, NBP, E), F32)
    xs_s = ((3 * NBK, COLS), BF)
    xg_s = ((384, COLS), BF)
    xq_s = ((192, COLS), BF)
    sends = [terms_s, face_s, face_s, ((32, WIDE), F32), ((128, WIDE), F32)]
    fetched = [
        ((NV, NB, E), F32),
        ((3, NB, NB), F32),
        ((NF, 4, NB), F32),
        ((3, NF, NF), F32),
        ((1, SLOTS), jnp.int32),
        base_s,
        ((3 * NBP, NBK), F32),
        ((4 * NFP, NBK), F32),
        xs_s,
        pltpu.SemaphoreType.DMA((11,)),
    ]
    begun = call(
        opening,
        constants + sends,
        fetched,
        raw + [jnp.full((1, E), odd, jnp.int32)],
        raw=11,
    )
    neighbour, cluster, orient = begun[:3]
    stiff, proj, star, nflux, lflux, lift_a, lift_b, own_lift, far, pick = begun[3:13]
    terms, d_hi, d_lo, p_swap, p_rest = begun[13:]
    thin_s = ((ORDER, 3, NBP, E), F32)
    thin_columns = 3 * E
    for step in range(STEPS):
        odd_step = step % 2 == 1
        if odd_step:
            nsum, fresh, d_hi, d_lo, p_swap, p_rest = call(
                functools.partial(critical, False, step),
                [nsum_s, thin_s] + sends[1:],
                [xg_s, xs_s, ((3 * NBK, thin_columns), BF)],
                [came, nsum, base, nflux, lift_a, lift_b, orient, far, stiff, thin_star, proj, pick, cluster, terms],
            )
        elif step > 0:
            nsum, terms, d_hi, d_lo, p_swap, p_rest = call(
                functools.partial(critical, False, step),
                [nsum_s] + sends,
                [xg_s, xs_s],
                [came, nsum, base, nflux, lift_a, lift_b, orient, far, stiff, star, proj, pick, cluster, terms],
            )
        swapped = lax.ppermute(p_swap, "dom", chip)
        side = functools.partial(beside, step)
        if step == 0:
            nsum, base, thin_star, thin_lflux = call(
                side,
                [nsum_s, base_s, ((21, 3, E), F32), ((21, 4, E), F32)],
                [xs_s, xq_s],
                [terms, d_hi, d_lo, neighbour, stiff, star, proj, lflux, own_lift, cluster],
            )
        elif odd_step:
            nsum, base = call(
                side,
                [nsum_s, base_s],
                [((3 * NBK, thin_columns), BF), ((192, thin_columns), BF)],
                [fresh, d_hi, d_lo, neighbour, stiff, thin_star, proj, thin_lflux, own_lift, cluster, nsum, base],
            )
        else:
            nsum, base = call(
                side,
                [nsum_s, base_s],
                [xs_s, xq_s],
                [terms, d_hi, d_lo, neighbour, stiff, star, proj, lflux, own_lift, cluster, nsum, base],
            )
        swapped = swapped.reshape(4, H, WIDE)
        swapped = jnp.where(holds_swapped, jnp.concatenate([swapped, swapped]), 0.0)
        p_rest = p_rest.reshape(8, 16, WIDE)
        block = jnp.concatenate([p_rest[:, 0:H], swapped], axis=1)
        block, nsum, base = lax.optimization_barrier((block, nsum, base))
        came = lax.cond(at_end, within_line, across_pair, block).reshape(128, WIDE)
    (out,) = call(
        functools.partial(critical, True, STEPS),
        [((NV, NB, E), F32)],
        [xg_s],
        [came, nsum, base, nflux, lift_a, lift_b, orient, far],
    )
    return jnp.transpose(out, (1, 0, 2))


def solution(mesh):
    placed = (
        P(None, None, ("dom", "sub")),
        P(),
        P(None, None, None, ("dom", "sub")),
        P(None, None, None, ("dom", "sub")),
        P(None, None, None, ("dom", "sub")),
        P(),
        P(),
        P(("dom", "sub")),
        P(None, ("dom", "sub")),
        P(None, ("dom", "sub")),
        P("dom", "sub", None),
    )
    return jax.shard_map(
        body, mesh=mesh, in_specs=placed, out_specs=P(None, None, ("dom", "sub")), check_vma=False
    )
```

profile of v0, /device:TPU:24, one launch (start us, length us, event | category | flops | bytes accessed | tf_op | source)
XLA Modules:
  0.0 130.3 jit_solution(1707697917681919365)
XLA Ops:
  0.0 4.8 %shard_map.109 = (s32[4,128]{1,0:T(4,128)S(1)}, s32[1,128]{1,0:T(1,128)S(1)}, s32[4,128]{1,0:T(4,128)S(1)}, bf16[120,144]{1,0:T(8,128)(2,1)S(1)}, bf16[64,144]{1...) custom-call(s32[1,96]{1,0:T(1,128)} %bitcast.77, ...), custom_call_target="tpu_custom_call" | custom-call | tf_op jit(solution)/shard_map/pallas_call | solution.py:416
  4.9 1.3 %shard_map.110 = (f32[144,512]{1,0:T(8,128)S(1)}, f32[9,40,128]{2,1,0:T(8,128)S(1)}, f32[21,3,128]{2,1,0:T(4,128)S(1)}, f32[21,4,128]{2,1,0:T(4,128)S(1)}) custom-call(f32[5,9,40,128]{3,2,1,0:T(8,128)S(1)} %get-tuple-element.197.refs_0_.refs_13_, bf16[144,512]{1,0:T(8,128)(2,1)S(1)} %get-tuple-element.198.refs_1_, ...), custom_call_target="tpu_custom_call" | custom-call | tf_op jit(solution)/shard_map/pallas_call | solution.py:416
  6.4 14.8 %conditional.8 = (f32[128,144]{1,0:T(8,128)S(1)}) conditional(s32[]{:T(128)} %convert_element_type.2, f32[8,16,144]{2,1,0:T(8,128)S(1)} %pad_maximum_fusion.8, (s32[]{:T(128)}, f32[8,16,144]{2,1,0:T(8,128)S(1)}) %tuple.78), branch_computations={%region_0.1_spmd, %region_1.2_spmd} | conditional | flops 27649 | bytes 294930 | solution.py:556
  6.4 14.8 %all_to_all.64 = f32[8,16,144]{2,1,0:T(8,128)S(1)} all-to-all(f32[8,16,144]{2,1,0:T(8,128)S(1)} %param), channel_id=1, replica_groups={{4,5,6,7,8,9,10,11},{12,13,14,15,16,17,18,19},{20,21,22,23,24,25,26,27}..., dimensions={0} | all-to-all | bytes 147456 | tf_op jit(solution)/shard_map/cond/branch_0_fun/all_to_all | solution.py:438
  21.2 3.1 %shard_map.111 = (f32[144,512]{1,0:T(8,128)S(1)}, f32[5,3,40,128]{3,2,1,0:T(8,128)S(1)}, bf16[144,512]{1,0:T(8,128)(2,1)S(1)}, bf16[144,512]{1,0:T(8,128)(2,1)S(...) custom-call(f32[128,144]{1,0:T(8,128)S(1)} %get-tuple-element.297.refs_0_, f32[144,512]{1,0:T(8,128)S(1)} %get-tuple-element.210.refs_1_, ...), custom_call_target="tpu_custom_call" | custom-call | tf_op jit(solution)/shard_map/pallas_call | solution.py:416
  24.4 1.1 shard_map.112
  25.7 10.6 %conditional.9 = (f32[128,144]{1,0:T(8,128)S(1)}) conditional(s32[]{:T(128)} %convert_element_type.2, f32[8,16,144]{2,1,0:T(8,128)S(1)} %pad_maximum_fusion.9, (s32[]{:T(128)}, f32[8,16,144]{2,1,0:T(8,128)S(1)}) %tuple.80), branch_computations={%region_2.3_spmd, %region_3.4_spmd} | conditional | flops 27649 | bytes 294930 | solution.py:556
  25.7 10.6 %all_to_all.66 = f32[8,16,144]{2,1,0:T(8,128)S(1)} all-to-all(f32[8,16,144]{2,1,0:T(8,128)S(1)} %param.2), channel_id=1, replica_groups={{4,5,6,7,8,9,10,11},{12,13,14,15,16,17,18,19},{20,21,22,23,24,25,26,27}..., dimensions={0} | all-to-all | bytes 147456 | tf_op jit(solution)/shard_map/cond/branch_0_fun/all_to_all | solution.py:438
  36.3 3.5 %shard_map.113 = (f32[144,512]{1,0:T(8,128)S(1)}, f32[5,9,40,128]{3,2,1,0:T(8,128)S(1)}, bf16[144,512]{1,0:T(8,128)(2,1)S(1)}, bf16[144,512]{1,0:T(8,128)(2,1)S(...) custom-call(f32[128,144]{1,0:T(8,128)S(1)} %get-tuple-element.298.refs_0_, f32[144,512]{1,0:T(8,128)S(1)} %get-tuple-element.229.refs_1_, ...), custom_call_target="tpu_custom_call" | custom-call | tf_op jit(solution)/shard_map/pallas_call | solution.py:416
  40.1 1.3 %shard_map.114 = (f32[144,512]{1,0:T(8,128)S(1)}, f32[9,40,128]{2,1,0:T(8,128)S(1)}) custom-call(f32[5,9,40,128]{3,2,1,0:T(8,128)S(1)} %get-tuple-element.233.refs_0_.refs_13_, bf16[144,512]{1,0:T(8,128)(2,1)S(1)} %get-tuple-element.234.refs_1_, bf16[144,512]{1,0:T(8,128)(2,1)S(1)} %get-tuple-element.235.refs_2_, s32[4,128]{1,0:T(4,128)S(1)} %get-tuple-element.200.refs_3_, ...), custom_call_target="tpu_custom_call" | custom-call | tf_op jit(solution)/shard_map/pallas_call | solution.py:416
  41.6 10.6 %conditional.10 = (f32[128,144]{1,0:T(8,128)S(1)}) conditional(s32[]{:T(128)} %convert_element_type.2, f32[8,16,144]{2,1,0:T(8,128)S(1)} %pad_maximum_fusion.10, (s32[]{:T(128)}, f32[8,16,144]{2,1,0:T(8,128)S(1)}) %tuple.82), branch_computations={%region_4.5_spmd, %region_5.6_spmd} | conditional | flops 27649 | bytes 294930 | solution.py:556
  41.6 10.6 %all_to_all.68 = f32[8,16,144]{2,1,0:T(8,128)S(1)} all-to-all(f32[8,16,144]{2,1,0:T(8,128)S(1)} %param.4), channel_id=1, replica_groups={{4,5,6,7,8,9,10,11},{12,13,14,15,16,17,18,19},{20,21,22,23,24,25,26,27}..., dimensions={0} | all-to-all | bytes 147456 | tf_op jit(solution)/shard_map/cond/branch_0_fun/all_to_all | solution.py:438
  52.2 3.1 %shard_map.115 = (f32[144,512]{1,0:T(8,128)S(1)}, f32[5,3,40,128]{3,2,1,0:T(8,128)S(1)}, bf16[144,512]{1,0:T(8,128)(2,1)S(1)}, bf16[144,512]{1,0:T(8,128)(2,1)S(...) custom-call(f32[128,144]{1,0:T(8,128)S(1)} %get-tuple-element.299.refs_0_, f32[144,512]{1,0:T(8,128)S(1)} %get-tuple-element.240.refs_1_, ...), custom_call_target="tpu_custom_call" | custom-call | tf_op jit(solution)/shard_map/pallas_call | solution.py:416
  55.4 1.1 shard_map.116
  56.6 10.6 %conditional.11 = (f32[128,144]{1,0:T(8,128)S(1)}) conditional(s32[]{:T(128)} %convert_element_type.2, f32[8,16,144]{2,1,0:T(8,128)S(1)} %pad_maximum_fusion.11, (s32[]{:T(128)}, f32[8,16,144]{2,1,0:T(8,128)S(1)}) %tuple.84), branch_computations={%region_6.7_spmd, %region_7.8_spmd} | conditional | flops 27649 | bytes 294930 | solution.py:556
  56.6 10.6 %all_to_all.70 = f32[8,16,144]{2,1,0:T(8,128)S(1)} all-to-all(f32[8,16,144]{2,1,0:T(8,128)S(1)} %param.6), channel_id=1, replica_groups={{4,5,6,7,8,9,10,11},{12,13,14,15,16,17,18,19},{20,21,22,23,24,25,26,27}..., dimensions={0} | all-to-all | bytes 147456 | tf_op jit(solution)/shard_map/cond/branch_0_fun/all_to_all | solution.py:438
  67.2 3.5 %shard_map.117 = (f32[144,512]{1,0:T(8,128)S(1)}, f32[5,9,40,128]{3,2,1,0:T(8,128)S(1)}, bf16[144,512]{1,0:T(8,128)(2,1)S(1)}, bf16[144,512]{1,0:T(8,128)(2,1)S(...) custom-call(f32[128,144]{1,0:T(8,128)S(1)} %get-tuple-element.300.refs_0_, f32[144,512]{1,0:T(8,128)S(1)} %get-tuple-element.251.refs_1_, ...), custom_call_target="tpu_custom_call" | custom-call | tf_op jit(solution)/shard_map/pallas_call | solution.py:416
  70.9 1.3 %shard_map.118 = (f32[144,512]{1,0:T(8,128)S(1)}, f32[9,40,128]{2,1,0:T(8,128)S(1)}) custom-call(f32[5,9,40,128]{3,2,1,0:T(8,128)S(1)} %get-tuple-element.255.refs_0_.refs_13_, bf16[144,512]{1,0:T(8,128)(2,1)S(1)} %get-tuple-element.256.refs_1_, bf16[144,512]{1,0:T(8,128)(2,1)S(1)} %get-tuple-element.257.refs_2_, s32[4,128]{1,0:T(4,128)S(1)} %get-tuple-element.200.refs_3_, ...), custom_call_target="tpu_custom_call" | custom-call | tf_op jit(solution)/shard_map/pallas_call | solution.py:416
  72.3 10.6 %conditional.12 = (f32[128,144]{1,0:T(8,128)S(1)}) conditional(s32[]{:T(128)} %convert_element_type.2, f32[8,16,144]{2,1,0:T(8,128)S(1)} %pad_maximum_fusion.12, (s32[]{:T(128)}, f32[8,16,144]{2,1,0:T(8,128)S(1)}) %tuple.86), branch_computations={%region_8.9_spmd, %region_9.10_spmd} | conditional | flops 27649 | bytes 294930 | solution.py:556
  72.3 10.6 %all_to_all.72 = f32[8,16,144]{2,1,0:T(8,128)S(1)} all-to-all(f32[8,16,144]{2,1,0:T(8,128)S(1)} %param.8), channel_id=1, replica_groups={{4,5,6,7,8,9,10,11},{12,13,14,15,16,17,18,19},{20,21,22,23,24,25,26,27}..., dimensions={0} | all-to-all | bytes 147456 | tf_op jit(solution)/shard_map/cond/branch_0_fun/all_to_all | solution.py:438
  82.9 3.1 %shard_map.119 = (f32[144,512]{1,0:T(8,128)S(1)}, f32[5,3,40,128]{3,2,1,0:T(8,128)S(1)}, bf16[144,512]{1,0:T(8,128)(2,1)S(1)}, bf16[144,512]{1,0:T(8,128)(2,1)S(...) custom-call(f32[128,144]{1,0:T(8,128)S(1)} %get-tuple-element.301.refs_0_, f32[144,512]{1,0:T(8,128)S(1)} %get-tuple-element.262.refs_1_, ...), custom_call_target="tpu_custom_call" | custom-call | tf_op jit(solution)/shard_map/pallas_call | solution.py:416
  86.1 1.1 shard_map.120
  87.4 10.6 %conditional.13 = (f32[128,144]{1,0:T(8,128)S(1)}) conditional(s32[]{:T(128)} %convert_element_type.2, f32[8,16,144]{2,1,0:T(8,128)S(1)} %pad_maximum_fusion.13, (s32[]{:T(128)}, f32[8,16,144]{2,1,0:T(8,128)S(1)}) %tuple.88), branch_computations={%region_10.11_spmd, %region_11.12_spmd} | conditional | flops 27649 | bytes 294930 | solution.py:556
  87.4 10.6 %all_to_all.74 = f32[8,16,144]{2,1,0:T(8,128)S(1)} all-to-all(f32[8,16,144]{2,1,0:T(8,128)S(1)} %param.10), channel_id=1, replica_groups={{4,5,6,7,8,9,10,11},{12,13,14,15,16,17,18,19},{20,21,22,23,24,25,26,27}..., dimensions={0} | all-to-all | bytes 147456 | tf_op jit(solution)/shard_map/cond/branch_0_fun/all_to_all | solution.py:438
  98.0 3.5 %shard_map.121 = (f32[144,512]{1,0:T(8,128)S(1)}, f32[5,9,40,128]{3,2,1,0:T(8,128)S(1)}, bf16[144,512]{1,0:T(8,128)(2,1)S(1)}, bf16[144,512]{1,0:T(8,128)(2,1)S(...) custom-call(f32[128,144]{1,0:T(8,128)S(1)} %get-tuple-element.302.refs_0_, f32[144,512]{1,0:T(8,128)S(1)} %get-tuple-element.273.refs_1_, ...), custom_call_target="tpu_custom_call" | custom-call | tf_op jit(solution)/shard_map/pallas_call | solution.py:416
  101.7 1.3 %shard_map.122 = (f32[144,512]{1,0:T(8,128)S(1)}, f32[9,40,128]{2,1,0:T(8,128)S(1)}) custom-call(f32[5,9,40,128]{3,2,1,0:T(8,128)S(1)} %get-tuple-element.277.refs_0_.refs_13_, bf16[144,512]{1,0:T(8,128)(2,1)S(1)} %get-tuple-element.278.refs_1_, bf16[144,512]{1,0:T(8,128)(2,1)S(1)} %get-tuple-element.279.refs_2_, s32[4,128]{1,0:T(4,128)S(1)} %get-tuple-element.200.refs_3_, ...), custom_call_target="tpu_custom_call" | custom-call | tf_op jit(solution)/shard_map/pallas_call | solution.py:416
  103.1 10.6 %conditional.14 = (f32[128,144]{1,0:T(8,128)S(1)}) conditional(s32[]{:T(128)} %convert_element_type.2, f32[8,16,144]{2,1,0:T(8,128)S(1)} %pad_maximum_fusion.14, (s32[]{:T(128)}, f32[8,16,144]{2,1,0:T(8,128)S(1)}) %tuple.90), branch_computations={%region_12.13_spmd, %region_13.14_spmd} | conditional | flops 27649 | bytes 294930 | solution.py:556
  103.1 10.6 %all_to_all.76 = f32[8,16,144]{2,1,0:T(8,128)S(1)} all-to-all(f32[8,16,144]{2,1,0:T(8,128)S(1)} %param.12), channel_id=1, replica_groups={{4,5,6,7,8,9,10,11},{12,13,14,15,16,17,18,19},{20,21,22,23,24,25,26,27}..., dimensions={0} | all-to-all | bytes 147456 | tf_op jit(solution)/shard_map/cond/branch_0_fun/all_to_all | solution.py:438
  113.7 3.1 %shard_map.123 = (f32[144,512]{1,0:T(8,128)S(1)}, f32[5,3,40,128]{3,2,1,0:T(8,128)S(1)}, bf16[144,512]{1,0:T(8,128)(2,1)S(1)}, bf16[144,512]{1,0:T(8,128)(2,1)S(...) custom-call(f32[128,144]{1,0:T(8,128)S(1)} %get-tuple-element.303.refs_0_, f32[144,512]{1,0:T(8,128)S(1)} %get-tuple-element.284.refs_1_, ...), custom_call_target="tpu_custom_call" | custom-call | tf_op jit(solution)/shard_map/pallas_call | solution.py:416
  118.2 10.6 %conditional.15 = (f32[128,144]{1,0:T(8,128)S(1)}) conditional(s32[]{:T(128)} %convert_element_type.2, f32[8,16,144]{2,1,0:T(8,128)S(1)} %pad_maximum_fusion.15, (s32[]{:T(128)}, f32[8,16,144]{2,1,0:T(8,128)S(1)}) %tuple.92), branch_computations={%region_14.15_spmd, %region_15.16_spmd} | conditional | flops 27649 | bytes 294930 | solution.py:556
  118.2 10.6 %all_to_all.78 = f32[8,16,144]{2,1,0:T(8,128)S(1)} all-to-all(f32[8,16,144]{2,1,0:T(8,128)S(1)} %param.14), channel_id=1, replica_groups={{4,5,6,7,8,9,10,11},{12,13,14,15,16,17,18,19},{20,21,22,23,24,25,26,27}..., dimensions={0} | all-to-all | bytes 147456 | tf_op jit(solution)/shard_map/cond/branch_0_fun/all_to_all | solution.py:438
  128.8 1.5 %shard_map.125 = f32[9,35,128]{2,1,0:T(8,128)} custom-call(f32[128,144]{1,0:T(8,128)S(1)} %get-tuple-element.304.refs_0_, f32[144,512]{1,0:T(8,128)S(1)} %get-tuple-element.295.refs_1_, f32[9,40,128]{2,1,0:T(8,128)S(1)} %get-tuple-element.296.refs_2_, f32[9,9,4,128]{3,2,1,0:T(4,128)S(1)} %get-tuple-element.212.refs_3_, ...), custom_call_target="tpu_custom_call" | custom-call | tf_op jit(solution)/shard_map/pallas_call | solution.py:416
  (43 shorter events, 3.0 us)
Async XLA Ops:
  4.8 1.5 %collective-permute-start = (f32[32,144]{1,0:T(8,128)S(1)}, f32[32,144]{1,0:T(8,128)S(1)}, u32[]{:S(2)}, u32[]{:S(2)}) collective-permute-start(f32[32,144]{1,0:T(8,128)S(1)} %get-tuple-element.196), channel_id=1, source_target_pairs={{0,4},{4,0},{8,12},{12,8},{16,20},{20,16},{24,28},{28,24},{32,36},... | collective-permute-start | bytes 55304 | tf_op jit(solution)/shard_map/ppermute | solution.py:528
  24.3 1.3 collective-permute-start.1
  39.8 1.7 %collective-permute-start.2 = (f32[32,144]{1,0:T(8,128)S(1)}, f32[32,144]{1,0:T(8,128)S(1)}, u32[]{:S(2)}, u32[]{:S(2)}) collective-permute-start(f32[32,144]{1,0:T(8,128)S(1)} %get-tuple-element.232), channel_id=1, source_target_pairs={{0,4},{4,0},{8,12},{12,8},{16,20},{20,16},{24,28},{28,24},{32,36},... | collective-permute-start | bytes 55304 | tf_op jit(solution)/shard_map/ppermute | solution.py:528
  55.2 1.3 collective-permute-start.3
  70.8 1.4 %collective-permute-start.4 = (f32[32,144]{1,0:T(8,128)S(1)}, f32[32,144]{1,0:T(8,128)S(1)}, u32[]{:S(2)}, u32[]{:S(2)}) collective-permute-start(f32[32,144]{1,0:T(8,128)S(1)} %get-tuple-element.254), channel_id=1, source_target_pairs={{0,4},{4,0},{8,12},{12,8},{16,20},{20,16},{24,28},{28,24},{32,36},... | collective-permute-start | bytes 55304 | tf_op jit(solution)/shard_map/ppermute | solution.py:528
  86.0 1.3 collective-permute-start.5
  101.5 1.5 %collective-permute-start.6 = (f32[32,144]{1,0:T(8,128)S(1)}, f32[32,144]{1,0:T(8,128)S(1)}, u32[]{:S(2)}, u32[]{:S(2)}) collective-permute-start(f32[32,144]{1,0:T(8,128)S(1)} %get-tuple-element.276), channel_id=1, source_target_pairs={{0,4},{4,0},{8,12},{12,8},{16,20},{20,16},{24,28},{28,24},{32,36},... | collective-permute-start | bytes 55304 | tf_op jit(solution)/shard_map/ppermute | solution.py:528
  116.8 1.3 collective-permute-start.7
where the time goes:
time: 131 us; the launch traced here: 130 us
  blocking collectives  89 us (68%)
  Pallas kernels  38.9 us (30%)
    all_to_all x8, blocking collectives, exchange(): lax.all_to_all(block, ('dom', 'sub'), split_axis=0, concat_axis=0, tiled=...  89 us
    pallas_call x17, Pallas kernels, call(): pl.pallas_call(kernel, out_shape=[jax.ShapeDtypeStruct(s, t) for s, t in...  38.9 us
  transfers between devices with their start and end apart: 8, of which 4 were waited for; matrix products, arithmetic and copies ran while one was open for 0% of the time, Pallas kernels for 8%

commit v1 on v0

--- a/solution.py
+++ b/solution.py
@@ -62,6 +62,14 @@
     return acc
 
 
+def gather(got_ref, row_codes):
+    got = jnp.concatenate(halves(got_ref[...]), axis=0)
+    rows = lax.broadcasted_iota(jnp.int32, (128, E), 0)
+    far = jnp.concatenate([(rows == row).astype(F32).astype(BF) for row in row_codes], axis=1)
+    far = jnp.concatenate([far, far], axis=0)
+    return lax.dot_general(got, far, (((0,), (0,)), ((), ())), preferred_element_type=F32)
+
+
 def lane_group(shape):
     return lax.broadcasted_iota(jnp.int32, shape, len(shape) - 1) >> 5
 
@@ -83,6 +91,14 @@
 
 def apart(parts):
     return [shifted(parts[v // 4], -(v % 4)) for v in range(NV)]
+
+
+def faces_side_by_side(rows):
+    group = lane_group((1, E))
+    joined = rows[0:1, :]
+    for i in range(1, 4):
+        joined = jnp.where(group == i, shifted(rows[i : i + 1, :], i), joined)
+    return joined
 
 
 def thin_matrices(full_ref, thin_ref):
@@ -148,9 +164,8 @@
     return rows, offset == 0
 
 
-def expand_thin(step, upd, cluster, stiff, thin, proj, pick, terms_in, terms, d_hi, d_lo, pay_swap, pay_rest, xs, xt):
+def expand_thin(step, current, cluster, stiff, thin, proj, pick, terms_in, terms, d_hi, d_lo, pay_swap, pay_rest, xs, xt):
     rows, start = weight_rows(cluster, step)
-    current = side_by_side(upd)
     fresh = [None] * 3
     for k in range(ORDER):
         if k > 0:
@@ -204,7 +219,7 @@
     take = lambda n: [refs.pop(0) for _ in range(n)]
     odd_ref = refs.pop(0)
     neighbour_ref, cluster, orient = take(3)
-    stiff, proj, star, nflux, lflux, lift_a, lift_b, own_lift, far, pick = take(10)
+    stiff, proj, star, nflux, lflux, lift_a, lift_b, own_lift, pick, small = take(10)
     terms, d_hi, d_lo, pay_swap, pay_rest = take(5)
     dofs_s, stiff_s, proj_s, rot_s, send_ref, state, wide_s, tall_s, xs, sems = take(10)
     targets = [send_ref, neighbour_ref, stiff_s, proj_s, rot_s, cluster, dofs_s, star, nflux, lflux, orient]
@@ -228,9 +243,9 @@
     row = jnp.where(block == 2 * (1 - odd), (cross + source) * 16 + place, (same + source) * 16 + place)
     row = jnp.where(block == 2 * odd, row + H, row)
     row = jnp.where((codes >= FACES) & (codes < FACES + 4 * SLOTS), row, -1)
-    rows, _ = grid((128, E))
-    for i in range(4):
-        far[:, i * E : (i + 1) * E] = (rows == row[i : i + 1, :]).astype(F32).astype(BF)
+    small[8:12, :] = row
+    small[0:1, :] = faces_side_by_side(codes)
+    small[5:6, :] = faces_side_by_side(row)
     rows, columns = grid((160, SLOTS))
     flag = odd[:, 0:1]
     rest = rows - 32
@@ -285,6 +300,10 @@
 
     for copy in copies[5:]:
         copy.wait()
+    for i in range(4):
+        turns = jnp.where(lane_group((1, E)) == 0, orient[i : i + 1, :], 0)
+        turns = turns + shifted(turns, 1)
+        small[1 + i : 2 + i, :] = turns + shifted(turns, 2)
     state[...] = jnp.zeros_like(state)
     for v in range(NV):
         state[v, 0:NB, :] = dofs_s[v]
@@ -295,20 +314,14 @@
 def critical(last, step, *refs):
     refs = list(refs)
     take = lambda n: [refs.pop(0) for _ in range(n)]
-    got_ref, nsum_ref, base_ref, nflux, lift_a, lift_b, orient, far = take(8)
+    got_ref, nsum_ref, base_ref, nflux, lift_a, lift_b, orient, small = take(8)
     if last:
         out_ref, xg = take(2)
     else:
         stiff, star, proj, pick, cluster, terms_in = take(6)
         nsum_out, terms, d_hi, d_lo, pay_swap, pay_rest, xg, xs = take(8)
-        if step % 2:
-            (xt,) = take(1)
-
-    got_hi, got_lo = halves(got_ref[...])
-    dims = (((0,), (0,)), ((), ()))
-    arrived = lax.dot_general(got_hi, far[...], dims, preferred_element_type=F32)
-    arrived = arrived + lax.dot_general(got_lo, far[...], dims, preferred_element_type=F32)
-    total = nsum_ref[...] + arrived
+
+    total = nsum_ref[...] + gather(got_ref, [small[8 + i : 9 + i, :] for i in range(4)])
     if not last:
         nsum_out[...] = total
     for i in range(4):
@@ -335,12 +348,41 @@
     if last:
         for v in range(NV):
             out_ref[v] = upd[v][0:NB]
-    elif step % 2:
-        expand_thin(
-            step, upd, cluster, stiff, star, proj, pick, terms_in, terms, d_hi, d_lo, pay_swap, pay_rest, xs, xt
-        )
     else:
         expand(step, False, upd, cluster, stiff, star, proj, pick, terms_in, terms, d_hi, d_lo, pay_swap, pay_rest, xs)
+
+
+def critical_thin(step, *refs):
+    got_ref, nsum_ref, base_ref, nflux, lift_a, lift_b, small, stiff, star, proj, pick, cluster, terms_in = refs[:13]
+    terms, d_hi, d_lo, pay_swap, pay_rest, xg, xs, xt = refs[13:]
+    total = nsum_ref[...] + gather(got_ref, [small[5:6, :]])
+    acc = [None] * NV
+    for u in range(NV):
+        part = total[u * NFP : (u + 1) * NFP, :]
+        for v in range(NV):
+            term = part * nflux[u * NV + v : u * NV + v + 1, :]
+            acc[v] = term if acc[v] is None else acc[v] + term
+    group = lane_group((NFP, E))
+    for i in range(4):
+        chosen = []
+        for o in range(3):
+            mask = (small[1 + i : 2 + i, :] == o).astype(F32)
+            chosen.append(jnp.broadcast_to(mask, (NFP, E)).astype(BF))
+        for j in range(3):
+            part = jnp.zeros((NFP, E), F32)
+            for g in range(min(4, NV - 4 * j)):
+                part = jnp.where(group == g, shifted(acc[4 * j + g], g - i), part)
+            hi, lo = halves(part)
+            cols = slice(j * E, (j + 1) * E)
+            for o in range(3):
+                row = (i * 3 + o) * NFP
+                xg[row : row + NFP, cols] = hi * chosen[o]
+                xg[192 + row : 192 + row + NFP, cols] = lo * chosen[o]
+    two = dot(lift_a[...], xg[0:192, :])
+    lifted = two[0:NBP] + two[NBP : 2 * NBP] + dot(lift_b[...], xg[192:384, :])
+    base = side_by_side([base_ref[v] for v in range(NV)])
+    upd = [base[j] + lifted[:, j * E : (j + 1) * E] for j in range(3)]
+    expand_thin(step, upd, cluster, stiff, star, proj, pick, terms_in, terms, d_hi, d_lo, pay_swap, pay_rest, xs, xt)
 
 
 def beside(step, *refs):
@@ -348,20 +390,37 @@
     take = lambda n: [refs.pop(0) for _ in range(n)]
     first, thin = step == 0, step % 2 == 1
     terms, d_hi, d_lo, neighbour, stiff, star, proj, lflux, own_lift, cluster = take(10)
-    if not first:
+    small = refs.pop(0)
+    if thin:
+        got_ref = refs.pop(0)
+    if first:
+        nflux = refs.pop(0)
+    else:
         nsum_ref, base_ref = take(2)
     nsum_out, base_out = take(2)
+    if not thin:
+        nsum_thin = refs.pop(0)
     if first:
-        thin_star, thin_lflux = take(2)
+        thin_star, thin_lflux, thin_nflux = take(3)
     xs, xq = take(2)
     _, start = weight_rows(cluster, step)
     period = jnp.left_shift(jnp.int32(1), cluster[...]).astype(F32)
     face_rows = lax.broadcasted_iota(jnp.int32, (FACES, E), 0)
+    if thin:
+        arrived = gather(got_ref, [small[8 + i : 9 + i, :] for i in range(4)])
     for i in range(4):
         cols = slice(i * E, (i + 1) * E)
         near = (face_rows == neighbour[i : i + 1, :]).astype(F32).astype(BF)
         gathered = dot(d_hi[...], near) + dot(d_lo[...], near)
-        nsum_out[:, cols] = gathered if first else gathered + jnp.where(start, 0.0, nsum_ref[:, cols])
+        if not first:
+            kept = nsum_ref[:, cols]
+            if thin:
+                kept = kept + arrived[:, cols]
+            gathered = gathered + jnp.where(start, 0.0, kept)
+        nsum_out[:, cols] = gathered
+    if not thin:
+        near = (face_rows == small[0:1, :]).astype(F32).astype(BF)
+        nsum_thin[...] = dot(d_hi[...], near) + dot(d_lo[...], near)
     wide = 3 if thin else NV
     held = [[terms[k, v] for v in range(wide)] for k in range(ORDER)]
     if thin:
@@ -407,6 +466,9 @@
     if first:
         thin_matrices(star, thin_star)
         thin_matrices(lflux, thin_lflux)
+        for u in range(NV):
+            for v in range(NV):
+                thin_nflux[u * NV + v : u * NV + v + 1, :] = faces_side_by_side(nflux[u, v])
 
 
 def call(kernel, outs, scratch, args, raw=0):
@@ -474,8 +536,8 @@
         ((2 * NBP, 192), BF),
         ((NBP, 192), BF),
         ((NBP, 192), BF),
-        ((128, FACES), BF),
         ((160, FACES), BF),
+        ((16, E), jnp.int32),
     ]
     terms_s = ((ORDER, NV, NBP, E), F32)
     face_s = ((WIDE, FACES), BF)
@@ -505,60 +567,66 @@
         raw=11,
     )
     neighbour, cluster, orient = begun[:3]
-    stiff, proj, star, nflux, lflux, lift_a, lift_b, own_lift, far, pick = begun[3:13]
+    stiff, proj, star, nflux, lflux, lift_a, lift_b, own_lift, pick, small = begun[3:13]
     terms, d_hi, d_lo, p_swap, p_rest = begun[13:]
     thin_s = ((ORDER, 3, NBP, E), F32)
     thin_columns = 3 * E
     for step in range(STEPS):
         odd_step = step % 2 == 1
         if odd_step:
-            nsum, fresh, d_hi, d_lo, p_swap, p_rest = call(
-                functools.partial(critical, False, step),
-                [nsum_s, thin_s] + sends[1:],
-                [xg_s, xs_s, ((3 * NBK, thin_columns), BF)],
-                [came, nsum, base, nflux, lift_a, lift_b, orient, far, stiff, thin_star, proj, pick, cluster, terms],
+            fresh, d_hi, d_lo, p_swap, p_rest = call(
+                functools.partial(critical_thin, step),
+                [thin_s] + sends[1:],
+                [((384, thin_columns), BF), xs_s, ((3 * NBK, thin_columns), BF)],
+                [came, nsum_thin, base, thin_nflux, lift_a, lift_b, small]
+                + [stiff, thin_star, proj, pick, cluster, terms],
             )
         elif step > 0:
             nsum, terms, d_hi, d_lo, p_swap, p_rest = call(
                 functools.partial(critical, False, step),
                 [nsum_s] + sends,
                 [xg_s, xs_s],
-                [came, nsum, base, nflux, lift_a, lift_b, orient, far, stiff, star, proj, pick, cluster, terms],
+                [came, nsum, base, nflux, lift_a, lift_b, orient, small, stiff, star, proj, pick, cluster, terms],
             )
         swapped = lax.ppermute(p_swap, "dom", chip)
         side = functools.partial(beside, step)
+        thin_nsum_s = ((WIDE, E), F32)
         if step == 0:
-            nsum, base, thin_star, thin_lflux = call(
+            nsum, base, nsum_thin, thin_star, thin_lflux, thin_nflux = call(
                 side,
-                [nsum_s, base_s, ((21, 3, E), F32), ((21, 4, E), F32)],
+                [nsum_s, base_s, thin_nsum_s, ((21, 3, E), F32), ((21, 4, E), F32), ((NV * NV, E), F32)],
                 [xs_s, xq_s],
-                [terms, d_hi, d_lo, neighbour, stiff, star, proj, lflux, own_lift, cluster],
+                [terms, d_hi, d_lo, neighbour, stiff, star, proj, lflux, own_lift, cluster, small, nflux],
             )
         elif odd_step:
             nsum, base = call(
                 side,
                 [nsum_s, base_s],
                 [((3 * NBK, thin_columns), BF), ((192, thin_columns), BF)],
-                [fresh, d_hi, d_lo, neighbour, stiff, thin_star, proj, thin_lflux, own_lift, cluster, nsum, base],
+                [fresh, d_hi, d_lo, neighbour, stiff, thin_star, proj, thin_lflux, own_lift, cluster]
+                + [small, came, nsum, base],
             )
         else:
-            nsum, base = call(
+            nsum, base, nsum_thin = call(
                 side,
-                [nsum_s, base_s],
+                [nsum_s, base_s, thin_nsum_s],
                 [xs_s, xq_s],
-                [terms, d_hi, d_lo, neighbour, stiff, star, proj, lflux, own_lift, cluster, nsum, base],
+                [terms, d_hi, d_lo, neighbour, stiff, star, proj, lflux, own_lift, cluster, small, nsum, base],
             )
         swapped = swapped.reshape(4, H, WIDE)
         swapped = jnp.where(holds_swapped, jnp.concatenate([swapped, swapped]), 0.0)
         p_rest = p_rest.reshape(8, 16, WIDE)
         block = jnp.concatenate([p_rest[:, 0:H], swapped], axis=1)
-        block, nsum, base = lax.optimization_barrier((block, nsum, base))
+        if odd_step:
+            block, nsum, base = lax.optimization_barrier((block, nsum, base))
+        else:
+            block, nsum, base, nsum_thin = lax.optimization_barrier((block, nsum, base, nsum_thin))
         came = lax.cond(at_end, within_line, across_pair, block).reshape(128, WIDE)
     (out,) = call(
         functools.partial(critical, True, STEPS),
         [((NV, NB, E), F32)],
         [xg_s],
-        [came, nsum, base, nflux, lift_a, lift_b, orient, far],
+        [came, nsum, base, nflux, lift_a, lift_b, orient, small],
     )
     return jnp.transpose(out, (1, 0, 2))
 

time: 131 us -> 130 us (level)
  transfers between devices with their start and end apart: 8 -> 8, of which waited for: 4 -> 0; matrix products, arithmetic and copies ran while one was open for 0% -> 0% of each run, Pallas kernels for 8% -> 8%
where the time goes in v1:
time: 130 us; the launch traced here: 129 us
  blocking collectives  89 us (68%)
  Pallas kernels  37.8 us (29%)
    all_to_all x8, blocking collectives, exchange(): lax.all_to_all(block, ('dom', 'sub'), split_axis=0, concat_axis=0, tiled=...  89 us
    pallas_call x17, Pallas kernels, call(): pl.pallas_call(kernel, out_shape=[jax.ShapeDtypeStruct(s, t) for s, t in...  37.8 us
  transfers between devices with their start and end apart: 8, of which 0 were waited for; matrix products, arithmetic and copies ran while one was open for 0% of the time, Pallas kernels for 8%

profile of v1, /device:TPU:24, one launch (start us, length us, event | category | flops | bytes accessed | tf_op | source)
XLA Modules:
  0.0 129.1 jit_solution(1245055790907362117)
XLA Ops:
  0.0 4.7 %shard_map.109 = (s32[4,128]{1,0:T(4,128)S(1)}, s32[1,128]{1,0:T(1,128)S(1)}, s32[4,128]{1,0:T(4,128)S(1)}, bf16[120,144]{1,0:T(8,128)(2,1)S(1)}, bf16[64,144]{1...) custom-call(s32[1,96]{1,0:T(1,128)} %bitcast.77, ...), custom_call_target="tpu_custom_call" | custom-call | tf_op jit(solution)/shard_map/pallas_call | solution.py:478
  4.9 1.6 %shard_map.110 = (f32[144,512]{1,0:T(8,128)S(1)}, f32[9,40,128]{2,1,0:T(8,128)S(1)}, f32[144,128]{1,0:T(8,128)S(1)}, f32[21,3,128]{2,1,0:T(4,128)S(1)}, f32[21,4...) custom-call(f32[5,9,40,128]{3,2,1,0:T(8,128)S(1)} %get-tuple-element.202.refs_0_.refs_12_.refs_13_, ...), custom_call_target="tpu_custom_call" | custom-call | tf_op jit(solution)/shard_map/pallas_call | solution.py:478
  6.6 14.8 %conditional.8 = (f32[128,144]{1,0:T(8,128)S(1)}) conditional(s32[]{:T(128)} %convert_element_type.2, f32[8,16,144]{2,1,0:T(8,128)S(1)} %pad_maximum_fusion.8, (s32[]{:T(128)}, f32[8,16,144]{2,1,0:T(8,128)S(1)}) %tuple.78), branch_computations={%region_0.1_spmd, %region_1.2_spmd} | conditional | flops 27649 | bytes 294930 | solution.py:624
  6.6 14.8 %all_to_all.64 = f32[8,16,144]{2,1,0:T(8,128)S(1)} all-to-all(f32[8,16,144]{2,1,0:T(8,128)S(1)} %param), channel_id=1, replica_groups={{4,5,6,7,8,9,10,11},{12,13,14,15,16,17,18,19},{20,21,22,23,24,25,26,27}..., dimensions={0} | all-to-all | bytes 147456 | tf_op jit(solution)/shard_map/cond/branch_0_fun/all_to_all | solution.py:500
  21.4 2.6 %shard_map.111 = (f32[5,3,40,128]{3,2,1,0:T(8,128)S(1)}, bf16[144,512]{1,0:T(8,128)(2,1)S(1)}, bf16[144,512]{1,0:T(8,128)(2,1)S(1)}, f32[32,144]{1,0:T(8,128)S(1)}, f32[128,144]{1,0:T(8,128)S(1)}) custom-call(f32[128,144]{1,0:T(8,128)S(1)} %get-tuple-element.307.refs_0_.refs_11_, f32[144,128]{1,0:T(8,128)S(1)} %get-tuple-element.218.refs_1_, ...), custom_call_target="tpu_custom_call" | custom-call | tf_op jit(solution)/shard_map/pallas_call | solution.py:478
  24.2 1.2 shard_map.112
  25.5 10.6 %conditional.9 = (f32[128,144]{1,0:T(8,128)S(1)}) conditional(s32[]{:T(128)} %convert_element_type.2, f32[8,16,144]{2,1,0:T(8,128)S(1)} %pad_maximum_fusion.9, (s32[]{:T(128)}, f32[8,16,144]{2,1,0:T(8,128)S(1)}) %tuple.80), branch_computations={%region_2.3_spmd, %region_3.4_spmd} | conditional | flops 27649 | bytes 294930 | solution.py:624
  25.5 10.6 %all_to_all.66 = f32[8,16,144]{2,1,0:T(8,128)S(1)} all-to-all(f32[8,16,144]{2,1,0:T(8,128)S(1)} %param.2), channel_id=1, replica_groups={{4,5,6,7,8,9,10,11},{12,13,14,15,16,17,18,19},{20,21,22,23,24,25,26,27}..., dimensions={0} | all-to-all | bytes 147456 | tf_op jit(solution)/shard_map/cond/branch_0_fun/all_to_all | solution.py:500
  36.1 3.5 %shard_map.113 = (f32[144,512]{1,0:T(8,128)S(1)}, f32[5,9,40,128]{3,2,1,0:T(8,128)S(1)}, bf16[144,512]{1,0:T(8,128)(2,1)S(1)}, bf16[144,512]{1,0:T(8,128)(2,1)S(...) custom-call(f32[128,144]{1,0:T(8,128)S(1)} %get-tuple-element.308.refs_0_, f32[144,512]{1,0:T(8,128)S(1)} %get-tuple-element.235.refs_1_, ...), custom_call_target="tpu_custom_call" | custom-call | tf_op jit(solution)/shard_map/pallas_call | solution.py:478
  39.9 1.4 %shard_map.114 = (f32[144,512]{1,0:T(8,128)S(1)}, f32[9,40,128]{2,1,0:T(8,128)S(1)}, f32[144,128]{1,0:T(8,128)S(1)}) custom-call(f32[5,9,40,128]{3,2,1,0:T(8,128)S(1)} %get-tuple-element.240.refs_0_.refs_12_.refs_13_, bf16[144,512]{1,0:T(8,128)(2,1)S(1)} %get-tuple-element.241.refs_1_, bf16[144,512]{1,0:T(8,128)(2,1)S(1)} %get-tuple-element.242.refs_2_, ...), custom_call_target="tpu_custom_call" | custom-call | tf_op jit(solution)/shard_map/pallas_call | solution.py:478
  41.4 10.6 %conditional.10 = (f32[128,144]{1,0:T(8,128)S(1)}) conditional(s32[]{:T(128)} %convert_element_type.2, f32[8,16,144]{2,1,0:T(8,128)S(1)} %pad_maximum_fusion.10, (s32[]{:T(128)}, f32[8,16,144]{2,1,0:T(8,128)S(1)}) %tuple.82), branch_computations={%region_4.5_spmd, %region_5.6_spmd} | conditional | flops 27649 | bytes 294930 | solution.py:624
  41.4 10.6 %all_to_all.68 = f32[8,16,144]{2,1,0:T(8,128)S(1)} all-to-all(f32[8,16,144]{2,1,0:T(8,128)S(1)} %param.4), channel_id=1, replica_groups={{4,5,6,7,8,9,10,11},{12,13,14,15,16,17,18,19},{20,21,22,23,24,25,26,27}..., dimensions={0} | all-to-all | bytes 147456 | tf_op jit(solution)/shard_map/cond/branch_0_fun/all_to_all | solution.py:500
  52.0 2.6 %shard_map.115 = (f32[5,3,40,128]{3,2,1,0:T(8,128)S(1)}, bf16[144,512]{1,0:T(8,128)(2,1)S(1)}, bf16[144,512]{1,0:T(8,128)(2,1)S(1)}, f32[32,144]{1,0:T(8,128)S(1)}, f32[128,144]{1,0:T(8,128)S(1)}) custom-call(f32[128,144]{1,0:T(8,128)S(1)} %get-tuple-element.309.refs_0_.refs_11_, f32[144,128]{1,0:T(8,128)S(1)} %get-tuple-element.248.refs_1_, ...), custom_call_target="tpu_custom_call" | custom-call | tf_op jit(solution)/shard_map/pallas_call | solution.py:478
  56.0 10.6 %conditional.11 = (f32[128,144]{1,0:T(8,128)S(1)}) conditional(s32[]{:T(128)} %convert_element_type.2, f32[8,16,144]{2,1,0:T(8,128)S(1)} %pad_maximum_fusion.11, (s32[]{:T(128)}, f32[8,16,144]{2,1,0:T(8,128)S(1)}) %tuple.84), branch_computations={%region_6.7_spmd, %region_7.8_spmd} | conditional | flops 27649 | bytes 294930 | solution.py:624
  56.1 10.6 %all_to_all.70 = f32[8,16,144]{2,1,0:T(8,128)S(1)} all-to-all(f32[8,16,144]{2,1,0:T(8,128)S(1)} %param.6), channel_id=1, replica_groups={{4,5,6,7,8,9,10,11},{12,13,14,15,16,17,18,19},{20,21,22,23,24,25,26,27}..., dimensions={0} | all-to-all | bytes 147456 | tf_op jit(solution)/shard_map/cond/branch_0_fun/all_to_all | solution.py:500
  66.7 3.4 %shard_map.117 = (f32[144,512]{1,0:T(8,128)S(1)}, f32[5,9,40,128]{3,2,1,0:T(8,128)S(1)}, bf16[144,512]{1,0:T(8,128)(2,1)S(1)}, bf16[144,512]{1,0:T(8,128)(2,1)S(...) custom-call(f32[128,144]{1,0:T(8,128)S(1)} %get-tuple-element.310.refs_0_, f32[144,512]{1,0:T(8,128)S(1)} %get-tuple-element.259.refs_1_, ...), custom_call_target="tpu_custom_call" | custom-call | tf_op jit(solution)/shard_map/pallas_call | solution.py:478
  70.2 1.4 %shard_map.118 = (f32[144,512]{1,0:T(8,128)S(1)}, f32[9,40,128]{2,1,0:T(8,128)S(1)}, f32[144,128]{1,0:T(8,128)S(1)}) custom-call(f32[5,9,40,128]{3,2,1,0:T(8,128)S(1)} %get-tuple-element.263.refs_0_.refs_12_.refs_13_, bf16[144,512]{1,0:T(8,128)(2,1)S(1)} %get-tuple-element.264.refs_1_, bf16[144,512]{1,0:T(8,128)(2,1)S(1)} %get-tuple-element.265.refs_2_, ...), custom_call_target="tpu_custom_call" | custom-call | tf_op jit(solution)/shard_map/pallas_call | solution.py:478
  71.8 10.6 %conditional.12 = (f32[128,144]{1,0:T(8,128)S(1)}) conditional(s32[]{:T(128)} %convert_element_type.2, f32[8,16,144]{2,1,0:T(8,128)S(1)} %pad_maximum_fusion.12, (s32[]{:T(128)}, f32[8,16,144]{2,1,0:T(8,128)S(1)}) %tuple.86), branch_computations={%region_8.9_spmd, %region_9.10_spmd} | conditional | flops 27649 | bytes 294930 | solution.py:624
  71.8 10.6 %all_to_all.72 = f32[8,16,144]{2,1,0:T(8,128)S(1)} all-to-all(f32[8,16,144]{2,1,0:T(8,128)S(1)} %param.8), channel_id=1, replica_groups={{4,5,6,7,8,9,10,11},{12,13,14,15,16,17,18,19},{20,21,22,23,24,25,26,27}..., dimensions={0} | all-to-all | bytes 147456 | tf_op jit(solution)/shard_map/cond/branch_0_fun/all_to_all | solution.py:500
  82.4 2.6 %shard_map.119 = (f32[5,3,40,128]{3,2,1,0:T(8,128)S(1)}, bf16[144,512]{1,0:T(8,128)(2,1)S(1)}, bf16[144,512]{1,0:T(8,128)(2,1)S(1)}, f32[32,144]{1,0:T(8,128)S(1)}, f32[128,144]{1,0:T(8,128)S(1)}) custom-call(f32[128,144]{1,0:T(8,128)S(1)} %get-tuple-element.311.refs_0_.refs_11_, f32[144,128]{1,0:T(8,128)S(1)} %get-tuple-element.271.refs_1_, ...), custom_call_target="tpu_custom_call" | custom-call | tf_op jit(solution)/shard_map/pallas_call | solution.py:478
  85.4 1.2 shard_map.120
  86.7 10.6 %conditional.13 = (f32[128,144]{1,0:T(8,128)S(1)}) conditional(s32[]{:T(128)} %convert_element_type.2, f32[8,16,144]{2,1,0:T(8,128)S(1)} %pad_maximum_fusion.13, (s32[]{:T(128)}, f32[8,16,144]{2,1,0:T(8,128)S(1)}) %tuple.88), branch_computations={%region_10.11_spmd, %region_11.12_spmd} | conditional | flops 27649 | bytes 294930 | solution.py:624
  86.7 10.6 %all_to_all.74 = f32[8,16,144]{2,1,0:T(8,128)S(1)} all-to-all(f32[8,16,144]{2,1,0:T(8,128)S(1)} %param.10), channel_id=1, replica_groups={{4,5,6,7,8,9,10,11},{12,13,14,15,16,17,18,19},{20,21,22,23,24,25,26,27}..., dimensions={0} | all-to-all | bytes 147456 | tf_op jit(solution)/shard_map/cond/branch_0_fun/all_to_all | solution.py:500
  97.3 3.5 %shard_map.121 = (f32[144,512]{1,0:T(8,128)S(1)}, f32[5,9,40,128]{3,2,1,0:T(8,128)S(1)}, bf16[144,512]{1,0:T(8,128)(2,1)S(1)}, bf16[144,512]{1,0:T(8,128)(2,1)S(...) custom-call(f32[128,144]{1,0:T(8,128)S(1)} %get-tuple-element.312.refs_0_, f32[144,512]{1,0:T(8,128)S(1)} %get-tuple-element.282.refs_1_, ...), custom_call_target="tpu_custom_call" | custom-call | tf_op jit(solution)/shard_map/pallas_call | solution.py:478
  100.8 1.4 %shard_map.122 = (f32[144,512]{1,0:T(8,128)S(1)}, f32[9,40,128]{2,1,0:T(8,128)S(1)}, f32[144,128]{1,0:T(8,128)S(1)}) custom-call(f32[5,9,40,128]{3,2,1,0:T(8,128)S(1)} %get-tuple-element.286.refs_0_.refs_12_, bf16[144,512]{1,0:T(8,128)(2,1)S(1)} %get-tuple-element.287.refs_1_, bf16[144,512]{1,0:T(8,128)(2,1)S(1)} %get-tuple-element.288.refs_2_, ...), custom_call_target="tpu_custom_call" | custom-call | tf_op jit(solution)/shard_map/pallas_call | solution.py:478
  102.4 10.6 %conditional.14 = (f32[128,144]{1,0:T(8,128)S(1)}) conditional(s32[]{:T(128)} %convert_element_type.2, f32[8,16,144]{2,1,0:T(8,128)S(1)} %pad_maximum_fusion.14, (s32[]{:T(128)}, f32[8,16,144]{2,1,0:T(8,128)S(1)}) %tuple.90), branch_computations={%region_12.13_spmd, %region_13.14_spmd} | conditional | flops 27649 | bytes 294930 | solution.py:624
  102.4 10.6 %all_to_all.76 = f32[8,16,144]{2,1,0:T(8,128)S(1)} all-to-all(f32[8,16,144]{2,1,0:T(8,128)S(1)} %param.12), channel_id=1, replica_groups={{4,5,6,7,8,9,10,11},{12,13,14,15,16,17,18,19},{20,21,22,23,24,25,26,27}..., dimensions={0} | all-to-all | bytes 147456 | tf_op jit(solution)/shard_map/cond/branch_0_fun/all_to_all | solution.py:500
  113.0 2.6 %shard_map.123 = (f32[5,3,40,128]{3,2,1,0:T(8,128)S(1)}, bf16[144,512]{1,0:T(8,128)(2,1)S(1)}, bf16[144,512]{1,0:T(8,128)(2,1)S(1)}, f32[32,144]{1,0:T(8,128)S(1)}, f32[128,144]{1,0:T(8,128)S(1)}) custom-call(f32[128,144]{1,0:T(8,128)S(1)} %get-tuple-element.313.refs_0_.refs_11_, f32[144,128]{1,0:T(8,128)S(1)} %get-tuple-element.294.refs_1_, ...), custom_call_target="tpu_custom_call" | custom-call | tf_op jit(solution)/shard_map/pallas_call | solution.py:478
  115.7 1.2 shard_map.124
  117.1 10.6 %conditional.15 = (f32[128,144]{1,0:T(8,128)S(1)}) conditional(s32[]{:T(128)} %convert_element_type.2, f32[8,16,144]{2,1,0:T(8,128)S(1)} %pad_maximum_fusion.15, (s32[]{:T(128)}, f32[8,16,144]{2,1,0:T(8,128)S(1)}) %tuple.92), branch_computations={%region_14.15_spmd, %region_15.16_spmd} | conditional | flops 27649 | bytes 294930 | solution.py:624
  117.1 10.6 %all_to_all.78 = f32[8,16,144]{2,1,0:T(8,128)S(1)} all-to-all(f32[8,16,144]{2,1,0:T(8,128)S(1)} %param.14), channel_id=1, replica_groups={{4,5,6,7,8,9,10,11},{12,13,14,15,16,17,18,19},{20,21,22,23,24,25,26,27}..., dimensions={0} | all-to-all | bytes 147456 | tf_op jit(solution)/shard_map/cond/branch_0_fun/all_to_all | solution.py:500
  127.7 1.5 %shard_map.125 = f32[9,35,128]{2,1,0:T(8,128)} custom-call(f32[128,144]{1,0:T(8,128)S(1)} %get-tuple-element.314.refs_0_, f32[144,512]{1,0:T(8,128)S(1)} %get-tuple-element.305.refs_1_, f32[9,40,128]{2,1,0:T(8,128)S(1)} %get-tuple-element.306.refs_2_, f32[9,9,4,128]{3,2,1,0:T(4,128)S(1)} %get-tuple-element.213.refs_11_.refs_3_, ...), custom_call_target="tpu_custom_call" | custom-call | tf_op jit(solution)/shard_map/pallas_call | solution.py:478
  (43 shorter events, 3.1 us)
Async XLA Ops:
  4.8 1.7 %collective-permute-start = (f32[32,144]{1,0:T(8,128)S(1)}, f32[32,144]{1,0:T(8,128)S(1)}, u32[]{:S(2)}, u32[]{:S(2)}) collective-permute-start(f32[32,144]{1,0:T(8,128)S(1)} %get-tuple-element.201), channel_id=1, source_target_pairs={{0,4},{4,0},{8,12},{12,8},{16,20},{20,16},{24,28},{28,24},{32,36},... | collective-permute-start | bytes 55304 | tf_op jit(solution)/shard_map/ppermute | solution.py:591
  24.0 1.3 %collective-permute-start.1 = (f32[32,144]{1,0:T(8,128)S(1)}, f32[32,144]{1,0:T(8,128)S(1)}, u32[]{:S(2)}, u32[]{:S(2)}) collective-permute-start(f32[32,144]{1,0:T(8,128)S(1)} %get-tuple-element.226), channel_id=1, source_target_pairs={{0,4},{4,0},{8,12},{12,8},{16,20},{20,16},{24,28},{28,24},{32,36},... | collective-permute-start | bytes 55304 | tf_op jit(solution)/shard_map/ppermute | solution.py:591
  39.6 1.7 %collective-permute-start.2 = (f32[32,144]{1,0:T(8,128)S(1)}, f32[32,144]{1,0:T(8,128)S(1)}, u32[]{:S(2)}, u32[]{:S(2)}) collective-permute-start(f32[32,144]{1,0:T(8,128)S(1)} %get-tuple-element.239), channel_id=1, source_target_pairs={{0,4},{4,0},{8,12},{12,8},{16,20},{20,16},{24,28},{28,24},{32,36},... | collective-permute-start | bytes 55304 | tf_op jit(solution)/shard_map/ppermute | solution.py:591
  54.6 1.3 %collective-permute-start.3 = (f32[32,144]{1,0:T(8,128)S(1)}, f32[32,144]{1,0:T(8,128)S(1)}, u32[]{:S(2)}, u32[]{:S(2)}) collective-permute-start(f32[32,144]{1,0:T(8,128)S(1)} %get-tuple-element.251), channel_id=1, source_target_pairs={{0,4},{4,0},{8,12},{12,8},{16,20},{20,16},{24,28},{28,24},{32,36},... | collective-permute-start | bytes 55304 | tf_op jit(solution)/shard_map/ppermute | solution.py:591
  70.1 1.6 %collective-permute-start.4 = (f32[32,144]{1,0:T(8,128)S(1)}, f32[32,144]{1,0:T(8,128)S(1)}, u32[]{:S(2)}, u32[]{:S(2)}) collective-permute-start(f32[32,144]{1,0:T(8,128)S(1)} %get-tuple-element.262), channel_id=1, source_target_pairs={{0,4},{4,0},{8,12},{12,8},{16,20},{20,16},{24,28},{28,24},{32,36},... | collective-permute-start | bytes 55304 | tf_op jit(solution)/shard_map/ppermute | solution.py:591
  85.0 1.5 %collective-permute-start.5 = (f32[32,144]{1,0:T(8,128)S(1)}, f32[32,144]{1,0:T(8,128)S(1)}, u32[]{:S(2)}, u32[]{:S(2)}) collective-permute-start(f32[32,144]{1,0:T(8,128)S(1)} %get-tuple-element.274), channel_id=1, source_target_pairs={{0,4},{4,0},{8,12},{12,8},{16,20},{20,16},{24,28},{28,24},{32,36},... | collective-permute-start | bytes 55304 | tf_op jit(solution)/shard_map/ppermute | solution.py:591
  100.7 1.5 %collective-permute-start.6 = (f32[32,144]{1,0:T(8,128)S(1)}, f32[32,144]{1,0:T(8,128)S(1)}, u32[]{:S(2)}, u32[]{:S(2)}) collective-permute-start(f32[32,144]{1,0:T(8,128)S(1)} %get-tuple-element.285), channel_id=1, source_target_pairs={{0,4},{4,0},{8,12},{12,8},{16,20},{20,16},{24,28},{28,24},{32,36},... | collective-permute-start | bytes 55304 | tf_op jit(solution)/shard_map/ppermute | solution.py:591
  115.6 1.3 %collective-permute-start.7 = (f32[32,144]{1,0:T(8,128)S(1)}, f32[32,144]{1,0:T(8,128)S(1)}, u32[]{:S(2)}, u32[]{:S(2)}) collective-permute-start(f32[32,144]{1,0:T(8,128)S(1)} %get-tuple-element.297), channel_id=1, source_target_pairs={{0,4},{4,0},{8,12},{12,8},{16,20},{20,16},{24,28},{28,24},{32,36},... | collective-permute-start | bytes 55304 | tf_op jit(solution)/shard_map/ppermute | solution.py:591

commit v2 on v1

--- a/solution.py
+++ b/solution.py
@@ -70,27 +70,33 @@
     return lax.dot_general(got, far, (((0,), (0,)), ((), ())), preferred_element_type=F32)
 
 
-def lane_group(shape):
-    return lax.broadcasted_iota(jnp.int32, shape, len(shape) - 1) >> 5
-
-
-def shifted(x, groups):
-    return x if groups % 4 == 0 else pltpu.roll(x, groups % 4 * 32, x.ndim - 1)
-
-
-def side_by_side(values):
-    group = lane_group(values[0].shape)
+def lane_group(shape, g=4):
+    return lax.broadcasted_iota(jnp.int32, shape, len(shape) - 1) // (E // g)
+
+
+def shifted(x, groups, g=4):
+    return x if groups % g == 0 else pltpu.roll(x, groups % g * (E // g), x.ndim - 1)
+
+
+def side_by_side(values, g=4):
+    group = lane_group(values[0].shape, g)
     parts = []
-    for j in range(3):
+    for j in range(-(-NV // g)):
         part = jnp.zeros_like(values[0])
-        for g in range(min(4, len(values) - 4 * j)):
-            part = jnp.where(group == g, shifted(values[4 * j + g], g), part)
+        for n in range(min(g, NV - g * j)):
+            part = jnp.where(group == n, shifted(values[g * j + n], n, g), part)
         parts.append(part)
     return parts
 
 
-def apart(parts):
-    return [shifted(parts[v // 4], -(v % 4)) for v in range(NV)]
+def apart(parts, g=4):
+    return [shifted(parts[v // g], -(v % g), g) for v in range(NV)]
+
+
+def over_groups(x, g):
+    for distance in (1, 2)[: g // 2]:
+        x = x + shifted(x, distance, g)
+    return x
 
 
 def faces_side_by_side(rows):
@@ -101,55 +107,57 @@
     return joined
 
 
-def thin_matrices(full_ref, thin_ref):
+def thin_matrices(full_ref, thin_ref, g=4):
+    whole = NV // g
     picks = []
-    for to in range(2):
-        for of in range(2):
-            for r in range(4):
-                picks.append([(4 * of + (g - r) % 4, 4 * to + g) for g in range(4)])
-    picks += [[(8, g) for g in range(4)], [(8, 4 + g) for g in range(4)]]
-    picks += [[(g, 8) for g in range(4)], [(4 + g, 8) for g in range(4)], [(8, 8)]]
+    for to in range(whole):
+        for of in range(whole):
+            for r in range(g):
+                picks.append([(g * of + (n - r) % g, g * to + n) for n in range(g)])
+    picks += [[(NV - 1, g * to + n) for n in range(g)] for to in range(whole)]
+    picks += [[(g * of + n, NV - 1) for n in range(g)] for of in range(whole)]
+    picks.append([(NV - 1, NV - 1)])
     depth = full_ref.shape[2]
-    group = lane_group((depth, E))
-    for n, sources in enumerate(picks):
+    group = lane_group((depth, E), g)
+    for k, sources in enumerate(picks):
         row = jnp.zeros((depth, E), F32)
-        for g, (u, v) in enumerate(sources):
-            row = jnp.where(group == g, shifted(full_ref[u, v], g), row)
-        thin_ref[n] = row
-
-
-def mix(acc, parts, thin_ref, d):
-    first, second, third = parts
-    spread = third + shifted(third, 1)
-    spread = spread + shifted(spread, 2)
-    terms = [[], [], []]
-    for r in range(4):
-        one, two = shifted(first, r), shifted(second, r)
-        for to in range(2):
-            terms[to].append(one * thin_ref[8 * to + r, d : d + 1, :])
-            terms[to].append(two * thin_ref[8 * to + 4 + r, d : d + 1, :])
-    for to in range(2):
-        terms[to].append(spread * thin_ref[16 + to, d : d + 1, :])
-    terms[2] = [part * thin_ref[18 + n, d : d + 1, :] for n, part in enumerate(parts)]
-    for to in range(3):
+        for n, (u, v) in enumerate(sources):
+            row = jnp.where(group == n, shifted(full_ref[u, v], n, g), row)
+        thin_ref[k] = row
+
+
+def mix(acc, parts, thin_ref, d, g=4):
+    whole = NV // g
+    spread = over_groups(parts[whole], g)
+    terms = [[] for _ in range(whole)]
+    for of in range(whole):
+        for r in range(g):
+            part = shifted(parts[of], r, g)
+            for to in range(whole):
+                terms[to].append(part * thin_ref[(to * whole + of) * g + r, d : d + 1, :])
+    base = whole * whole * g
+    for to in range(whole):
+        terms[to].append(spread * thin_ref[base + to, d : d + 1, :])
+    base = base + whole
+    terms.append([part * thin_ref[base + n, d : d + 1, :] for n, part in enumerate(parts)])
+    for to in range(whole + 1):
         for term in terms[to]:
             acc[to] = term if acc[to] is None else acc[to] + term
 
 
-def mixed_parts(acc):
-    last = acc[2] + shifted(acc[2], 2)
-    last = last + shifted(last, 1)
-    return [acc[0], acc[1], jnp.where(lane_group(last.shape) == 0, last, 0.0)]
-
-
-def derive_thin(parts, stiff_ref, thin_ref, xt_ref):
+def mixed_parts(acc, g=4):
+    last = over_groups(acc[-1], g)
+    return acc[:-1] + [jnp.where(lane_group(last.shape, g) == 0, last, 0.0)]
+
+
+def derive_thin(parts, stiff_ref, thin_ref, xt_ref, g=4):
     fill_basis(xt_ref, parts)
-    applied = dot(stiff_ref[...], xt_ref[...])
-    acc = [None] * 3
+    applied = dot(stiff_ref[...], xt_ref[:, 0 : len(parts) * E])
+    acc = [None] * len(parts)
     for d in range(3):
         rows = applied[d * NBP : (d + 1) * NBP]
-        mix(acc, [rows[:, j * E : (j + 1) * E] for j in range(3)], thin_ref, d)
-    return mixed_parts(acc)
+        mix(acc, [rows[:, j * E : (j + 1) * E] for j in range(len(parts))], thin_ref, d, g)
+    return mixed_parts(acc, g)
 
 
 def weight_rows(cluster_ref, step):
@@ -186,10 +194,14 @@
 
 def expand(step, first, upd, cluster, stiff, star, proj, pick, terms_in, terms, d_hi, d_lo, pay_swap, pay_rest, xs):
     rows, start = weight_rows(cluster, step)
+    paired = step % 4 == 2
     current = upd
     total = [None] * NV
     for k in range(ORDER):
-        if k > 0:
+        if paired:
+            parts = side_by_side(upd, 2) if k == 0 else derive_thin(parts, stiff, star, xs, 2)
+            current = upd if k == 0 else apart(parts, 2)
+        elif k > 0:
             current = derive(current, stiff, star, xs)
         for v in range(NV):
             kept = current[v] if first else jnp.where(start, current[v], terms_in[k, v])
@@ -211,7 +223,7 @@
     pay = lax.dot_general(pick[...], d_hi[...], dims, preferred_element_type=F32)
     pay = pay + lax.dot_general(pick[...], d_lo[...], dims, preferred_element_type=F32)
     pay_swap[...] = pay[0:32]
-    pay_rest[...] = pay[32:160]
+    pay_rest[...] = pay[32:96]
 
 
 def opening(*refs):
@@ -246,19 +258,18 @@
     small[8:12, :] = row
     small[0:1, :] = faces_side_by_side(codes)
     small[5:6, :] = faces_side_by_side(row)
-    rows, columns = grid((160, SLOTS))
+    rows, columns = grid((96, SLOTS))
     flag = odd[:, 0:1]
     rest = rows - 32
-    peer, place = rest >> 4, jnp.bitwise_and(rest, 15)
+    peer, place = rest >> 3, jnp.bitwise_and(rest, 7)
     inside = jnp.where((peer >> 2) == 1 - flag, 32, 64 * flag)
     wanted = inside + jnp.bitwise_and(peer, 3) * H + place
-    wanted = jnp.where(rest < 0, 64 * (1 - flag) + rows, jnp.where(place < H, wanted, -1))
+    wanted = jnp.where(rest < 0, 64 * (1 - flag) + rows, wanted)
     chooser = (columns == wanted).astype(F32)
     listed = jnp.broadcast_to(send_ref[...].astype(F32), (8, SLOTS))
     listed = lax.dot_general(chooser, listed, (((1,), (1,)), ((), ())), precision=high, preferred_element_type=F32)
-    listed = jnp.where(wanted[:, 0:1] < 0, float(FACES), listed[:, 0:1])
-    _, columns = grid((160, FACES))
-    pick[...] = (columns.astype(F32) == listed).astype(F32).astype(BF)
+    _, columns = grid((96, FACES))
+    pick[...] = (columns.astype(F32) == listed[:, 0:1]).astype(F32).astype(BF)
 
     for copy in copies[2:5]:
         copy.wait()
@@ -276,6 +287,14 @@
             tall_s[i * NFP + f : i * NFP + f + 1, 0:NB] = proj_s[f, i : i + 1, :]
     hi, lo = halves(tall_s[...])
     proj[...] = (dot(hi, twice) + dot(lo, once)).astype(BF)
+    for copy in copies[5:8]:
+        copy.wait()
+    state[...] = jnp.zeros_like(state)
+    for v in range(NV):
+        state[v, 0:NB, :] = dofs_s[v]
+    upd = [state[v] for v in range(NV)]
+    expand(0, True, upd, cluster, stiff, star, proj, pick, None, terms, d_hi, d_lo, pay_swap, pay_rest, xs)
+
     rows, columns = grid((64, 192))
     twice = ((columns == rows) | (columns == rows + 64)).astype(F32).astype(BF)
     once = (columns == rows + 128).astype(F32).astype(BF)
@@ -297,18 +316,12 @@
     lift_a[0:NBP, :] = hi
     lift_a[NBP : 2 * NBP, :] = lo
     lift_b[...] = hi
-
-    for copy in copies[5:]:
+    for copy in copies[8:]:
         copy.wait()
     for i in range(4):
         turns = jnp.where(lane_group((1, E)) == 0, orient[i : i + 1, :], 0)
         turns = turns + shifted(turns, 1)
         small[1 + i : 2 + i, :] = turns + shifted(turns, 2)
-    state[...] = jnp.zeros_like(state)
-    for v in range(NV):
-        state[v, 0:NB, :] = dofs_s[v]
-    upd = [state[v] for v in range(NV)]
-    expand(0, True, upd, cluster, stiff, star, proj, pick, None, terms, d_hi, d_lo, pay_swap, pay_rest, xs)
 
 
 def critical(last, step, *refs):
@@ -401,7 +414,7 @@
     if not thin:
         nsum_thin = refs.pop(0)
     if first:
-        thin_star, thin_lflux, thin_nflux = take(3)
+        thin_star, thin_lflux, thin_nflux, pair_star = take(4)
     xs, xq = take(2)
     _, start = weight_rows(cluster, step)
     period = jnp.left_shift(jnp.int32(1), cluster[...]).astype(F32)
@@ -466,6 +479,7 @@
     if first:
         thin_matrices(star, thin_star)
         thin_matrices(lflux, thin_lflux)
+        thin_matrices(star, pair_star, 2)
         for u in range(NV):
             for v in range(NV):
                 thin_nflux[u * NV + v : u * NV + v + 1, :] = faces_side_by_side(nflux[u, v])
@@ -508,7 +522,6 @@
         own = exchange(jnp.where(odd == 1, block[0:4], block[4:8]), lines)
         return jnp.concatenate([own, own])
 
-    holds_swapped = (jnp.arange(8, dtype=jnp.int32) // 4 == 1 - odd)[:, None, None]
     raw = [
         send_list.reshape(1, SLOTS),
         neighbour,
@@ -536,7 +549,7 @@
         ((2 * NBP, 192), BF),
         ((NBP, 192), BF),
         ((NBP, 192), BF),
-        ((160, FACES), BF),
+        ((96, FACES), BF),
         ((16, E), jnp.int32),
     ]
     terms_s = ((ORDER, NV, NBP, E), F32)
@@ -546,7 +559,7 @@
     xs_s = ((3 * NBK, COLS), BF)
     xg_s = ((384, COLS), BF)
     xq_s = ((192, COLS), BF)
-    sends = [terms_s, face_s, face_s, ((32, WIDE), F32), ((128, WIDE), F32)]
+    sends = [terms_s, face_s, face_s, ((32, WIDE), F32), ((64, WIDE), F32)]
     fetched = [
         ((NV, NB, E), F32),
         ((3, NB, NB), F32),
@@ -586,15 +599,17 @@
                 functools.partial(critical, False, step),
                 [nsum_s] + sends,
                 [xg_s, xs_s],
-                [came, nsum, base, nflux, lift_a, lift_b, orient, small, stiff, star, proj, pick, cluster, terms],
+                [came, nsum, base, nflux, lift_a, lift_b, orient, small, stiff]
+                + [pair_star if step % 4 == 2 else star, proj, pick, cluster, terms],
             )
         swapped = lax.ppermute(p_swap, "dom", chip)
         side = functools.partial(beside, step)
         thin_nsum_s = ((WIDE, E), F32)
         if step == 0:
-            nsum, base, nsum_thin, thin_star, thin_lflux, thin_nflux = call(
+            nsum, base, nsum_thin, thin_star, thin_lflux, thin_nflux, pair_star = call(
                 side,
-                [nsum_s, base_s, thin_nsum_s, ((21, 3, E), F32), ((21, 4, E), F32), ((NV * NV, E), F32)],
+                [nsum_s, base_s, thin_nsum_s, ((21, 3, E), F32), ((21, 4, E), F32), ((NV * NV, E), F32)]
+                + [((41, 3, E), F32)],
                 [xs_s, xq_s],
                 [terms, d_hi, d_lo, neighbour, stiff, star, proj, lflux, own_lift, cluster, small, nflux],
             )
@@ -614,9 +629,7 @@
                 [terms, d_hi, d_lo, neighbour, stiff, star, proj, lflux, own_lift, cluster, small, nsum, base],
             )
         swapped = swapped.reshape(4, H, WIDE)
-        swapped = jnp.where(holds_swapped, jnp.concatenate([swapped, swapped]), 0.0)
-        p_rest = p_rest.reshape(8, 16, WIDE)
-        block = jnp.concatenate([p_rest[:, 0:H], swapped], axis=1)
+        block = jnp.concatenate([p_rest.reshape(8, H, WIDE), jnp.concatenate([swapped, swapped])], axis=1)
         if odd_step:
             block, nsum, base = lax.optimization_barrier((block, nsum, base))
         else:

time: 130 us -> 128 us (0.985)
  no operation moved by 1% of the time
where the time goes in v2:
time: 128 us; the launch traced here: 127 us
  blocking collectives  89 us (70%)
  Pallas kernels  36.7 us (29%)
    all_to_all x8, blocking collectives, exchange(): lax.all_to_all(block, ('dom', 'sub'), split_axis=0, concat_axis=0, tiled=...  89 us
    pallas_call x17, Pallas kernels, call(): pl.pallas_call(kernel, out_shape=[jax.ShapeDtypeStruct(s, t) for s, t in...  36.7 us
  transfers between devices with their start and end apart: 8, of which 0 were waited for; matrix products, arithmetic and copies ran while one was open for 0% of the time, Pallas kernels for 8%

profile of v2, /device:TPU:24, one launch (start us, length us, event | category | flops | bytes accessed | tf_op | source)
XLA Modules:
  0.0 127.4 jit_solution(7871815181318278386)
XLA Ops:
  0.0 4.7 %shard_map.109 = (s32[4,128]{1,0:T(4,128)S(1)}, s32[1,128]{1,0:T(1,128)S(1)}, s32[4,128]{1,0:T(4,128)S(1)}, bf16[120,144]{1,0:T(8,128)(2,1)S(1)}, bf16[64,144]{1...) custom-call(s32[1,96]{1,0:T(1,128)} %bitcast.77, ...), custom_call_target="tpu_custom_call" | custom-call | tf_op jit(solution)/shard_map/pallas_call | solution.py:492
  4.9 1.6 %shard_map.110 = (f32[144,512]{1,0:T(8,128)S(1)}, f32[9,40,128]{2,1,0:T(8,128)S(1)}, f32[144,128]{1,0:T(8,128)S(1)}, f32[21,3,128]{2,1,0:T(4,128)S(1)}, f32[21,4...) custom-call(f32[5,9,40,128]{3,2,1,0:T(8,128)S(1)} %get-tuple-element.203.refs_0_.refs_12_.refs_13_, ...), custom_call_target="tpu_custom_call" | custom-call | tf_op jit(solution)/shard_map/pallas_call | solution.py:492
  6.5 14.8 %conditional.8 = (f32[128,144]{1,0:T(8,128)S(1)}) conditional(s32[]{:T(128)} %convert_element_type.2, f32[8,16,144]{2,1,0:T(8,128)S(1)} %maximum_maximum_fusion, (s32[]{:T(128)}, f32[8,16,144]{2,1,0:T(8,128)S(1)}) %tuple.78), branch_computations={%region_0.1_spmd, %region_1.2_spmd} | conditional | flops 27649 | bytes 294930 | solution.py:637
  6.5 14.8 %all_to_all.64 = f32[8,16,144]{2,1,0:T(8,128)S(1)} all-to-all(f32[8,16,144]{2,1,0:T(8,128)S(1)} %param), channel_id=1, replica_groups={{4,5,6,7,8,9,10,11},{12,13,14,15,16,17,18,19},{20,21,22,23,24,25,26,27}..., dimensions={0} | all-to-all | bytes 147456 | tf_op jit(solution)/shard_map/cond/branch_0_fun/all_to_all | solution.py:514
  21.3 2.6 %shard_map.111 = (f32[5,3,40,128]{3,2,1,0:T(8,128)S(1)}, bf16[144,512]{1,0:T(8,128)(2,1)S(1)}, bf16[144,512]{1,0:T(8,128)(2,1)S(1)}, f32[32,144]{1,0:T(8,128)S(1)}, f32[64,144]{1,0:T(8,128)S(1)}) custom-call(f32[128,144]{1,0:T(8,128)S(1)} %get-tuple-element.309.refs_0_.refs_11_, f32[144,128]{1,0:T(8,128)S(1)} %get-tuple-element.219.refs_1_, ...), custom_call_target="tpu_custom_call" | custom-call | tf_op jit(solution)/shard_map/pallas_call | solution.py:492
  25.3 10.6 %conditional.9 = (f32[128,144]{1,0:T(8,128)S(1)}) conditional(s32[]{:T(128)} %convert_element_type.2, f32[8,16,144]{2,1,0:T(8,128)S(1)} %maximum_maximum_fusion.1, (s32[]{:T(128)}, f32[8,16,144]{2,1,0:T(8,128)S(1)}) %tuple.80), branch_computations={%region_2.3_spmd, %region_3.4_spmd} | conditional | flops 27649 | bytes 294930 | solution.py:637
  25.3 10.6 %all_to_all.66 = f32[8,16,144]{2,1,0:T(8,128)S(1)} all-to-all(f32[8,16,144]{2,1,0:T(8,128)S(1)} %param.2), channel_id=1, replica_groups={{4,5,6,7,8,9,10,11},{12,13,14,15,16,17,18,19},{20,21,22,23,24,25,26,27}..., dimensions={0} | all-to-all | bytes 147456 | tf_op jit(solution)/shard_map/cond/branch_0_fun/all_to_all | solution.py:514
  35.9 3.0 %shard_map.113 = (f32[144,512]{1,0:T(8,128)S(1)}, f32[5,9,40,128]{3,2,1,0:T(8,128)S(1)}, bf16[144,512]{1,0:T(8,128)(2,1)S(1)}, bf16[144,512]{1,0:T(8,128)(2,1)S(...) custom-call(f32[128,144]{1,0:T(8,128)S(1)} %get-tuple-element.310.refs_0_, f32[144,512]{1,0:T(8,128)S(1)} %get-tuple-element.236.refs_1_, ...), custom_call_target="tpu_custom_call" | custom-call | tf_op jit(solution)/shard_map/pallas_call | solution.py:492
  39.1 1.4 %shard_map.114 = (f32[144,512]{1,0:T(8,128)S(1)}, f32[9,40,128]{2,1,0:T(8,128)S(1)}, f32[144,128]{1,0:T(8,128)S(1)}) custom-call(f32[5,9,40,128]{3,2,1,0:T(8,128)S(1)} %get-tuple-element.242.refs_0_.refs_12_.refs_13_, bf16[144,512]{1,0:T(8,128)(2,1)S(1)} %get-tuple-element.243.refs_1_, bf16[144,512]{1,0:T(8,128)(2,1)S(1)} %get-tuple-element.244.refs_2_, ...), custom_call_target="tpu_custom_call" | custom-call | tf_op jit(solution)/shard_map/pallas_call | solution.py:492
  40.6 10.6 %conditional.10 = (f32[128,144]{1,0:T(8,128)S(1)}) conditional(s32[]{:T(128)} %convert_element_type.2, f32[8,16,144]{2,1,0:T(8,128)S(1)} %maximum_maximum_fusion.2, (s32[]{:T(128)}, f32[8,16,144]{2,1,0:T(8,128)S(1)}) %tuple.82), branch_computations={%region_4.5_spmd, %region_5.6_spmd} | conditional | flops 27649 | bytes 294930 | solution.py:637
  40.6 10.6 %all_to_all.68 = f32[8,16,144]{2,1,0:T(8,128)S(1)} all-to-all(f32[8,16,144]{2,1,0:T(8,128)S(1)} %param.4), channel_id=1, replica_groups={{4,5,6,7,8,9,10,11},{12,13,14,15,16,17,18,19},{20,21,22,23,24,25,26,27}..., dimensions={0} | all-to-all | bytes 147456 | tf_op jit(solution)/shard_map/cond/branch_0_fun/all_to_all | solution.py:514
  51.2 2.6 %shard_map.115 = (f32[5,3,40,128]{3,2,1,0:T(8,128)S(1)}, bf16[144,512]{1,0:T(8,128)(2,1)S(1)}, bf16[144,512]{1,0:T(8,128)(2,1)S(1)}, f32[32,144]{1,0:T(8,128)S(1)}, f32[64,144]{1,0:T(8,128)S(1)}) custom-call(f32[128,144]{1,0:T(8,128)S(1)} %get-tuple-element.311.refs_0_.refs_11_, f32[144,128]{1,0:T(8,128)S(1)} %get-tuple-element.250.refs_1_, ...), custom_call_target="tpu_custom_call" | custom-call | tf_op jit(solution)/shard_map/pallas_call | solution.py:492
  53.9 1.2 shard_map.116
  55.1 10.6 %conditional.11 = (f32[128,144]{1,0:T(8,128)S(1)}) conditional(s32[]{:T(128)} %convert_element_type.2, f32[8,16,144]{2,1,0:T(8,128)S(1)} %maximum_maximum_fusion.3, (s32[]{:T(128)}, f32[8,16,144]{2,1,0:T(8,128)S(1)}) %tuple.84), branch_computations={%region_6.7_spmd, %region_7.8_spmd} | conditional | flops 27649 | bytes 294930 | solution.py:637
  55.2 10.6 %all_to_all.70 = f32[8,16,144]{2,1,0:T(8,128)S(1)} all-to-all(f32[8,16,144]{2,1,0:T(8,128)S(1)} %param.6), channel_id=1, replica_groups={{4,5,6,7,8,9,10,11},{12,13,14,15,16,17,18,19},{20,21,22,23,24,25,26,27}..., dimensions={0} | all-to-all | bytes 147456 | tf_op jit(solution)/shard_map/cond/branch_0_fun/all_to_all | solution.py:514
  65.8 3.5 %shard_map.117 = (f32[144,512]{1,0:T(8,128)S(1)}, f32[5,9,40,128]{3,2,1,0:T(8,128)S(1)}, bf16[144,512]{1,0:T(8,128)(2,1)S(1)}, bf16[144,512]{1,0:T(8,128)(2,1)S(...) custom-call(f32[128,144]{1,0:T(8,128)S(1)} %get-tuple-element.312.refs_0_, f32[144,512]{1,0:T(8,128)S(1)} %get-tuple-element.261.refs_1_, ...), custom_call_target="tpu_custom_call" | custom-call | tf_op jit(solution)/shard_map/pallas_call | solution.py:492
  69.3 1.4 %shard_map.118 = (f32[144,512]{1,0:T(8,128)S(1)}, f32[9,40,128]{2,1,0:T(8,128)S(1)}, f32[144,128]{1,0:T(8,128)S(1)}) custom-call(f32[5,9,40,128]{3,2,1,0:T(8,128)S(1)} %get-tuple-element.265.refs_0_.refs_12_.refs_13_, bf16[144,512]{1,0:T(8,128)(2,1)S(1)} %get-tuple-element.266.refs_1_, bf16[144,512]{1,0:T(8,128)(2,1)S(1)} %get-tuple-element.267.refs_2_, ...), custom_call_target="tpu_custom_call" | custom-call | tf_op jit(solution)/shard_map/pallas_call | solution.py:492
  70.8 10.6 %conditional.12 = (f32[128,144]{1,0:T(8,128)S(1)}) conditional(s32[]{:T(128)} %convert_element_type.2, f32[8,16,144]{2,1,0:T(8,128)S(1)} %maximum_maximum_fusion.4, (s32[]{:T(128)}, f32[8,16,144]{2,1,0:T(8,128)S(1)}) %tuple.86), branch_computations={%region_8.9_spmd, %region_9.10_spmd} | conditional | flops 27649 | bytes 294930 | solution.py:637
  70.8 10.6 %all_to_all.72 = f32[8,16,144]{2,1,0:T(8,128)S(1)} all-to-all(f32[8,16,144]{2,1,0:T(8,128)S(1)} %param.8), channel_id=1, replica_groups={{4,5,6,7,8,9,10,11},{12,13,14,15,16,17,18,19},{20,21,22,23,24,25,26,27}..., dimensions={0} | all-to-all | bytes 147456 | tf_op jit(solution)/shard_map/cond/branch_0_fun/all_to_all | solution.py:514
  81.4 2.6 %shard_map.119 = (f32[5,3,40,128]{3,2,1,0:T(8,128)S(1)}, bf16[144,512]{1,0:T(8,128)(2,1)S(1)}, bf16[144,512]{1,0:T(8,128)(2,1)S(1)}, f32[32,144]{1,0:T(8,128)S(1)}, f32[64,144]{1,0:T(8,128)S(1)}) custom-call(f32[128,144]{1,0:T(8,128)S(1)} %get-tuple-element.313.refs_0_.refs_11_, f32[144,128]{1,0:T(8,128)S(1)} %get-tuple-element.273.refs_1_, ...), custom_call_target="tpu_custom_call" | custom-call | tf_op jit(solution)/shard_map/pallas_call | solution.py:492
  84.3 1.2 shard_map.120
  85.6 10.6 %conditional.13 = (f32[128,144]{1,0:T(8,128)S(1)}) conditional(s32[]{:T(128)} %convert_element_type.2, f32[8,16,144]{2,1,0:T(8,128)S(1)} %maximum_maximum_fusion.5, (s32[]{:T(128)}, f32[8,16,144]{2,1,0:T(8,128)S(1)}) %tuple.88), branch_computations={%region_10.11_spmd, %region_11.12_spmd} | conditional | flops 27649 | bytes 294930 | solution.py:637
  85.6 10.6 %all_to_all.74 = f32[8,16,144]{2,1,0:T(8,128)S(1)} all-to-all(f32[8,16,144]{2,1,0:T(8,128)S(1)} %param.10), channel_id=1, replica_groups={{4,5,6,7,8,9,10,11},{12,13,14,15,16,17,18,19},{20,21,22,23,24,25,26,27}..., dimensions={0} | all-to-all | bytes 147456 | tf_op jit(solution)/shard_map/cond/branch_0_fun/all_to_all | solution.py:514
  96.2 3.0 %shard_map.121 = (f32[144,512]{1,0:T(8,128)S(1)}, f32[5,9,40,128]{3,2,1,0:T(8,128)S(1)}, bf16[144,512]{1,0:T(8,128)(2,1)S(1)}, bf16[144,512]{1,0:T(8,128)(2,1)S(...) custom-call(f32[128,144]{1,0:T(8,128)S(1)} %get-tuple-element.314.refs_0_, f32[144,512]{1,0:T(8,128)S(1)} %get-tuple-element.284.refs_1_, ...), custom_call_target="tpu_custom_call" | custom-call | tf_op jit(solution)/shard_map/pallas_call | solution.py:492
  99.3 1.4 %shard_map.122 = (f32[144,512]{1,0:T(8,128)S(1)}, f32[9,40,128]{2,1,0:T(8,128)S(1)}, f32[144,128]{1,0:T(8,128)S(1)}) custom-call(f32[5,9,40,128]{3,2,1,0:T(8,128)S(1)} %get-tuple-element.288.refs_0_.refs_12_, bf16[144,512]{1,0:T(8,128)(2,1)S(1)} %get-tuple-element.289.refs_1_, bf16[144,512]{1,0:T(8,128)(2,1)S(1)} %get-tuple-element.290.refs_2_, ...), custom_call_target="tpu_custom_call" | custom-call | tf_op jit(solution)/shard_map/pallas_call | solution.py:492
  100.7 10.6 %conditional.14 = (f32[128,144]{1,0:T(8,128)S(1)}) conditional(s32[]{:T(128)} %convert_element_type.2, f32[8,16,144]{2,1,0:T(8,128)S(1)} %maximum_maximum_fusion.6, (s32[]{:T(128)}, f32[8,16,144]{2,1,0:T(8,128)S(1)}) %tuple.90), branch_computations={%region_12.13_spmd, %region_13.14_spmd} | conditional | flops 27649 | bytes 294930 | solution.py:637
  100.7 10.6 %all_to_all.76 = f32[8,16,144]{2,1,0:T(8,128)S(1)} all-to-all(f32[8,16,144]{2,1,0:T(8,128)S(1)} %param.12), channel_id=1, replica_groups={{4,5,6,7,8,9,10,11},{12,13,14,15,16,17,18,19},{20,21,22,23,24,25,26,27}..., dimensions={0} | all-to-all | bytes 147456 | tf_op jit(solution)/shard_map/cond/branch_0_fun/all_to_all | solution.py:514
  111.3 2.6 %shard_map.123 = (f32[5,3,40,128]{3,2,1,0:T(8,128)S(1)}, bf16[144,512]{1,0:T(8,128)(2,1)S(1)}, bf16[144,512]{1,0:T(8,128)(2,1)S(1)}, f32[32,144]{1,0:T(8,128)S(1)}, f32[64,144]{1,0:T(8,128)S(1)}) custom-call(f32[128,144]{1,0:T(8,128)S(1)} %get-tuple-element.315.refs_0_.refs_11_, f32[144,128]{1,0:T(8,128)S(1)} %get-tuple-element.296.refs_1_, ...), custom_call_target="tpu_custom_call" | custom-call | tf_op jit(solution)/shard_map/pallas_call | solution.py:492
  114.0 1.2 shard_map.124
  115.3 10.6 %conditional.15 = (f32[128,144]{1,0:T(8,128)S(1)}) conditional(s32[]{:T(128)} %convert_element_type.2, f32[8,16,144]{2,1,0:T(8,128)S(1)} %maximum_maximum_fusion.7, (s32[]{:T(128)}, f32[8,16,144]{2,1,0:T(8,128)S(1)}) %tuple.92), branch_computations={%region_14.15_spmd, %region_15.16_spmd} | conditional | flops 27649 | bytes 294930 | solution.py:637
  115.3 10.6 %all_to_all.78 = f32[8,16,144]{2,1,0:T(8,128)S(1)} all-to-all(f32[8,16,144]{2,1,0:T(8,128)S(1)} %param.14), channel_id=1, replica_groups={{4,5,6,7,8,9,10,11},{12,13,14,15,16,17,18,19},{20,21,22,23,24,25,26,27}..., dimensions={0} | all-to-all | bytes 147456 | tf_op jit(solution)/shard_map/cond/branch_0_fun/all_to_all | solution.py:514
  125.9 1.5 %shard_map.125 = f32[9,35,128]{2,1,0:T(8,128)} custom-call(f32[128,144]{1,0:T(8,128)S(1)} %get-tuple-element.316.refs_0_, f32[144,512]{1,0:T(8,128)S(1)} %get-tuple-element.307.refs_1_, f32[9,40,128]{2,1,0:T(8,128)S(1)} %get-tuple-element.308.refs_2_, f32[9,9,4,128]{3,2,1,0:T(4,128)S(1)} %get-tuple-element.214.refs_11_.refs_3_, ...), custom_call_target="tpu_custom_call" | custom-call | tf_op jit(solution)/shard_map/pallas_call | solution.py:492
  (26 shorter events, 2.4 us)
Async XLA Ops:
  4.8 1.7 %collective-permute-start = (f32[32,144]{1,0:T(8,128)S(1)}, f32[32,144]{1,0:T(8,128)S(1)}, u32[]{:S(2)}, u32[]{:S(2)}) collective-permute-start(f32[32,144]{1,0:T(8,128)S(1)} %get-tuple-element.202), channel_id=1, source_target_pairs={{0,4},{4,0},{8,12},{12,8},{16,20},{20,16},{24,28},{28,24},{32,36},... | collective-permute-start | bytes 55304 | tf_op jit(solution)/shard_map/ppermute | solution.py:605
  24.0 1.3 %collective-permute-start.1 = (f32[32,144]{1,0:T(8,128)S(1)}, f32[32,144]{1,0:T(8,128)S(1)}, u32[]{:S(2)}, u32[]{:S(2)}) collective-permute-start(f32[32,144]{1,0:T(8,128)S(1)} %get-tuple-element.227), channel_id=1, source_target_pairs={{0,4},{4,0},{8,12},{12,8},{16,20},{20,16},{24,28},{28,24},{32,36},... | collective-permute-start | bytes 55304 | tf_op jit(solution)/shard_map/ppermute | solution.py:605
  38.9 1.7 %collective-permute-start.2 = (f32[32,144]{1,0:T(8,128)S(1)}, f32[32,144]{1,0:T(8,128)S(1)}, u32[]{:S(2)}, u32[]{:S(2)}) collective-permute-start(f32[32,144]{1,0:T(8,128)S(1)} %get-tuple-element.241), channel_id=1, source_target_pairs={{0,4},{4,0},{8,12},{12,8},{16,20},{20,16},{24,28},{28,24},{32,36},... | collective-permute-start | bytes 55304 | tf_op jit(solution)/shard_map/ppermute | solution.py:605
  53.8 1.3 %collective-permute-start.3 = (f32[32,144]{1,0:T(8,128)S(1)}, f32[32,144]{1,0:T(8,128)S(1)}, u32[]{:S(2)}, u32[]{:S(2)}) collective-permute-start(f32[32,144]{1,0:T(8,128)S(1)} %get-tuple-element.253), channel_id=1, source_target_pairs={{0,4},{4,0},{8,12},{12,8},{16,20},{20,16},{24,28},{28,24},{32,36},... | collective-permute-start | bytes 55304 | tf_op jit(solution)/shard_map/ppermute | solution.py:605
  69.2 1.6 %collective-permute-start.4 = (f32[32,144]{1,0:T(8,128)S(1)}, f32[32,144]{1,0:T(8,128)S(1)}, u32[]{:S(2)}, u32[]{:S(2)}) collective-permute-start(f32[32,144]{1,0:T(8,128)S(1)} %get-tuple-element.264), channel_id=1, source_target_pairs={{0,4},{4,0},{8,12},{12,8},{16,20},{20,16},{24,28},{28,24},{32,36},... | collective-permute-start | bytes 55304 | tf_op jit(solution)/shard_map/ppermute | solution.py:605
  84.0 1.5 %collective-permute-start.5 = (f32[32,144]{1,0:T(8,128)S(1)}, f32[32,144]{1,0:T(8,128)S(1)}, u32[]{:S(2)}, u32[]{:S(2)}) collective-permute-start(f32[32,144]{1,0:T(8,128)S(1)} %get-tuple-element.276), channel_id=1, source_target_pairs={{0,4},{4,0},{8,12},{12,8},{16,20},{20,16},{24,28},{28,24},{32,36},... | collective-permute-start | bytes 55304 | tf_op jit(solution)/shard_map/ppermute | solution.py:605
  99.2 1.5 %collective-permute-start.6 = (f32[32,144]{1,0:T(8,128)S(1)}, f32[32,144]{1,0:T(8,128)S(1)}, u32[]{:S(2)}, u32[]{:S(2)}) collective-permute-start(f32[32,144]{1,0:T(8,128)S(1)} %get-tuple-element.287), channel_id=1, source_target_pairs={{0,4},{4,0},{8,12},{12,8},{16,20},{20,16},{24,28},{28,24},{32,36},... | collective-permute-start | bytes 55304 | tf_op jit(solution)/shard_map/ppermute | solution.py:605
  113.9 1.3 %collective-permute-start.7 = (f32[32,144]{1,0:T(8,128)S(1)}, f32[32,144]{1,0:T(8,128)S(1)}, u32[]{:S(2)}, u32[]{:S(2)}) collective-permute-start(f32[32,144]{1,0:T(8,128)S(1)} %get-tuple-element.299), channel_id=1, source_target_pairs={{0,4},{4,0},{8,12},{12,8},{16,20},{20,16},{24,28},{28,24},{32,36},... | collective-permute-start | bytes 55304 | tf_op jit(solution)/shard_map/ppermute | solution.py:605

commit v3 on v2

--- a/solution.py
+++ b/solution.py
@@ -172,7 +172,7 @@
     return rows, offset == 0
 
 
-def expand_thin(step, current, cluster, stiff, thin, proj, pick, terms_in, terms, d_hi, d_lo, pay_swap, pay_rest, xs, xt):
+def expand_thin(step, current, cluster, stiff, thin, proj, pick, terms_in, terms, faced, pay_swap, pay_rest, xs, xt):
     rows, start = weight_rows(cluster, step)
     fresh = [None] * 3
     for k in range(ORDER):
@@ -189,10 +189,10 @@
         for k in range(1, ORDER):
             kept = kept + terms_in[k, v] * rows[k]
         total.append(jnp.where(start, fresh[v], kept))
-    send(total, proj, pick, d_hi, d_lo, pay_swap, pay_rest, xs)
-
-
-def expand(step, first, upd, cluster, stiff, star, proj, pick, terms_in, terms, d_hi, d_lo, pay_swap, pay_rest, xs):
+    send(total, proj, pick, faced, pay_swap, pay_rest, xs)
+
+
+def expand(step, first, upd, cluster, stiff, star, proj, pick, terms_in, terms, faced, pay_swap, pay_rest, xs):
     rows, start = weight_rows(cluster, step)
     paired = step % 4 == 2
     current = upd
@@ -208,20 +208,20 @@
             terms[k, v] = kept
             part = kept * rows[k]
             total[v] = part if k == 0 else total[v] + part
-    send(total, proj, pick, d_hi, d_lo, pay_swap, pay_rest, xs)
-
-
-def send(total, proj, pick, d_hi, d_lo, pay_swap, pay_rest, xs):
+    send(total, proj, pick, faced, pay_swap, pay_rest, xs)
+
+
+def send(total, proj, pick, faced, pay_swap, pay_rest, xs):
     fill_basis(xs, total)
     faces = dot(proj[...], xs[...])
     for i in range(4):
         for v in range(NV):
             hi, lo = halves(faces[i * NFP : (i + 1) * NFP, v * E : (v + 1) * E])
-            d_hi[v * NFP : (v + 1) * NFP, i * E : (i + 1) * E] = hi
-            d_lo[v * NFP : (v + 1) * NFP, i * E : (i + 1) * E] = lo
+            faced[v * NFP : (v + 1) * NFP, i * E : (i + 1) * E] = hi
+            faced[WIDE + v * NFP : WIDE + (v + 1) * NFP, i * E : (i + 1) * E] = lo
     dims = (((1,), (1,)), ((), ()))
-    pay = lax.dot_general(pick[...], d_hi[...], dims, preferred_element_type=F32)
-    pay = pay + lax.dot_general(pick[...], d_lo[...], dims, preferred_element_type=F32)
+    pay = lax.dot_general(pick[...], faced[0:WIDE, :], dims, preferred_element_type=F32)
+    pay = pay + lax.dot_general(pick[...], faced[WIDE : 2 * WIDE, :], dims, preferred_element_type=F32)
     pay_swap[...] = pay[0:32]
     pay_rest[...] = pay[32:96]
 
@@ -232,7 +232,7 @@
     odd_ref = refs.pop(0)
     neighbour_ref, cluster, orient = take(3)
     stiff, proj, star, nflux, lflux, lift_a, lift_b, own_lift, pick, small = take(10)
-    terms, d_hi, d_lo, pay_swap, pay_rest = take(5)
+    terms, faced, pay_swap, pay_rest = take(4)
     dofs_s, stiff_s, proj_s, rot_s, send_ref, state, wide_s, tall_s, xs, sems = take(10)
     targets = [send_ref, neighbour_ref, stiff_s, proj_s, rot_s, cluster, dofs_s, star, nflux, lflux, orient]
     copies = [pltpu.make_async_copy(raw[n], targets[n], sems.at[n]) for n in range(11)]
@@ -293,7 +293,7 @@
     for v in range(NV):
         state[v, 0:NB, :] = dofs_s[v]
     upd = [state[v] for v in range(NV)]
-    expand(0, True, upd, cluster, stiff, star, proj, pick, None, terms, d_hi, d_lo, pay_swap, pay_rest, xs)
+    expand(0, True, upd, cluster, stiff, star, proj, pick, None, terms, faced, pay_swap, pay_rest, xs)
 
     rows, columns = grid((64, 192))
     twice = ((columns == rows) | (columns == rows + 64)).astype(F32).astype(BF)
@@ -332,42 +332,45 @@
         out_ref, xg = take(2)
     else:
         stiff, star, proj, pick, cluster, terms_in = take(6)
-        nsum_out, terms, d_hi, d_lo, pay_swap, pay_rest, xg, xs = take(8)
+        nsum_out, terms, faced, pay_swap, pay_rest, xg, xs = take(7)
 
     total = nsum_ref[...] + gather(got_ref, [small[8 + i : 9 + i, :] for i in range(4)])
     if not last:
         nsum_out[...] = total
+    masks = []
     for i in range(4):
-        acc = [None] * NV
-        for u in range(NV):
-            part = total[u * NFP : (u + 1) * NFP, i * E : (i + 1) * E]
-            for v in range(NV):
-                term = part * nflux[u, v, i : i + 1, :]
-                acc[v] = term if acc[v] is None else acc[v] + term
-        chosen = []
-        for o in range(3):
-            mask = (orient[i : i + 1, :] == o).astype(F32)
-            chosen.append(jnp.broadcast_to(mask, (NFP, E)).astype(BF))
-        for v in range(NV):
-            hi, lo = halves(acc[v])
-            for o in range(3):
-                row = (i * 3 + o) * NFP
+        chosen = [(orient[i : i + 1, :] == o).astype(F32) for o in range(3)]
+        masks.append([jnp.broadcast_to(mask, (NFP, E)).astype(BF) for mask in chosen])
+    upd = []
+    for chunk in (range(0, 4), range(4, 8), range(8, 9)):
+        for i in range(4):
+            acc = {}
+            for u in range(NV):
+                part = total[u * NFP : (u + 1) * NFP, i * E : (i + 1) * E]
+                for v in chunk:
+                    term = part * nflux[u, v, i : i + 1, :]
+                    acc[v] = term if u == 0 else acc[v] + term
+            for v in chunk:
+                hi, lo = halves(acc[v])
                 cols = slice(v * E, (v + 1) * E)
-                xg[row : row + NFP, cols] = hi * chosen[o]
-                xg[192 + row : 192 + row + NFP, cols] = lo * chosen[o]
-    two = dot(lift_a[...], xg[0:192, :])
-    lifted = two[0:NBP] + two[NBP : 2 * NBP] + dot(lift_b[...], xg[192:384, :])
-    upd = [base_ref[v] + lifted[:, v * E : (v + 1) * E] for v in range(NV)]
+                for o in range(3):
+                    row = (i * 3 + o) * NFP
+                    xg[row : row + NFP, cols] = hi * masks[i][o]
+                    xg[192 + row : 192 + row + NFP, cols] = lo * masks[i][o]
+        cols = slice(chunk[0] * E, (chunk[-1] + 1) * E)
+        two = dot(lift_a[...], xg[0:192, cols])
+        lifted = two[0:NBP] + two[NBP : 2 * NBP] + dot(lift_b[...], xg[192:384, cols])
+        upd += [base_ref[v] + lifted[:, n * E : (n + 1) * E] for n, v in enumerate(chunk)]
     if last:
         for v in range(NV):
             out_ref[v] = upd[v][0:NB]
     else:
-        expand(step, False, upd, cluster, stiff, star, proj, pick, terms_in, terms, d_hi, d_lo, pay_swap, pay_rest, xs)
+        expand(step, False, upd, cluster, stiff, star, proj, pick, terms_in, terms, faced, pay_swap, pay_rest, xs)
 
 
 def critical_thin(step, *refs):
     got_ref, nsum_ref, base_ref, nflux, lift_a, lift_b, small, stiff, star, proj, pick, cluster, terms_in = refs[:13]
-    terms, d_hi, d_lo, pay_swap, pay_rest, xg, xs, xt = refs[13:]
+    terms, faced, pay_swap, pay_rest, xg, xs, xt = refs[13:]
     total = nsum_ref[...] + gather(got_ref, [small[5:6, :]])
     acc = [None] * NV
     for u in range(NV):
@@ -395,14 +398,14 @@
     lifted = two[0:NBP] + two[NBP : 2 * NBP] + dot(lift_b[...], xg[192:384, :])
     base = side_by_side([base_ref[v] for v in range(NV)])
     upd = [base[j] + lifted[:, j * E : (j + 1) * E] for j in range(3)]
-    expand_thin(step, upd, cluster, stiff, star, proj, pick, terms_in, terms, d_hi, d_lo, pay_swap, pay_rest, xs, xt)
+    expand_thin(step, upd, cluster, stiff, star, proj, pick, terms_in, terms, faced, pay_swap, pay_rest, xs, xt)
 
 
 def beside(step, *refs):
     refs = list(refs)
     take = lambda n: [refs.pop(0) for _ in range(n)]
     first, thin = step == 0, step % 2 == 1
-    terms, d_hi, d_lo, neighbour, stiff, star, proj, lflux, own_lift, cluster = take(10)
+    terms, faced, neighbour, stiff, star, proj, lflux, own_lift, cluster = take(9)
     small = refs.pop(0)
     if thin:
         got_ref = refs.pop(0)
@@ -419,21 +422,23 @@
     _, start = weight_rows(cluster, step)
     period = jnp.left_shift(jnp.int32(1), cluster[...]).astype(F32)
     face_rows = lax.broadcasted_iota(jnp.int32, (FACES, E), 0)
+    wanted = [neighbour[i : i + 1, :] for i in range(4)] + ([] if thin else [small[0:1, :]])
+    near = jnp.concatenate([(face_rows == row).astype(F32).astype(BF) for row in wanted], axis=1)
+    gathered = dot(faced[...], near)
+    gathered = gathered[0:WIDE] + gathered[WIDE : 2 * WIDE]
     if thin:
         arrived = gather(got_ref, [small[8 + i : 9 + i, :] for i in range(4)])
     for i in range(4):
         cols = slice(i * E, (i + 1) * E)
-        near = (face_rows == neighbour[i : i + 1, :]).astype(F32).astype(BF)
-        gathered = dot(d_hi[...], near) + dot(d_lo[...], near)
+        fresh = gathered[:, cols]
         if not first:
             kept = nsum_ref[:, cols]
             if thin:
                 kept = kept + arrived[:, cols]
-            gathered = gathered + jnp.where(start, 0.0, kept)
-        nsum_out[:, cols] = gathered
+            fresh = fresh + jnp.where(start, 0.0, kept)
+        nsum_out[:, cols] = fresh
     if not thin:
-        near = (face_rows == small[0:1, :]).astype(F32).astype(BF)
-        nsum_thin[...] = dot(d_hi[...], near) + dot(d_lo[...], near)
+        nsum_thin[...] = gathered[:, FACES : FACES + E]
     wide = 3 if thin else NV
     held = [[terms[k, v] for v in range(wide)] for k in range(ORDER)]
     if thin:
@@ -553,13 +558,13 @@
         ((16, E), jnp.int32),
     ]
     terms_s = ((ORDER, NV, NBP, E), F32)
-    face_s = ((WIDE, FACES), BF)
+    face_s = ((2 * WIDE, FACES), BF)
     nsum_s = ((WIDE, FACES), F32)
     base_s = ((NV, NBP, E), F32)
     xs_s = ((3 * NBK, COLS), BF)
     xg_s = ((384, COLS), BF)
     xq_s = ((192, COLS), BF)
-    sends = [terms_s, face_s, face_s, ((32, WIDE), F32), ((64, WIDE), F32)]
+    sends = [terms_s, face_s, ((32, WIDE), F32), ((64, WIDE), F32)]
     fetched = [
         ((NV, NB, E), F32),
         ((3, NB, NB), F32),
@@ -581,13 +586,13 @@
     )
     neighbour, cluster, orient = begun[:3]
     stiff, proj, star, nflux, lflux, lift_a, lift_b, own_lift, pick, small = begun[3:13]
-    terms, d_hi, d_lo, p_swap, p_rest = begun[13:]
+    terms, faced, p_swap, p_rest = begun[13:]
     thin_s = ((ORDER, 3, NBP, E), F32)
     thin_columns = 3 * E
     for step in range(STEPS):
         odd_step = step % 2 == 1
         if odd_step:
-            fresh, d_hi, d_lo, p_swap, p_rest = call(
+            fresh, faced, p_swap, p_rest = call(
                 functools.partial(critical_thin, step),
                 [thin_s] + sends[1:],
                 [((384, thin_columns), BF), xs_s, ((3 * NBK, thin_columns), BF)],
@@ -595,7 +600,7 @@
                 + [stiff, thin_star, proj, pick, cluster, terms],
             )
         elif step > 0:
-            nsum, terms, d_hi, d_lo, p_swap, p_rest = call(
+            nsum, terms, faced, p_swap, p_rest = call(
                 functools.partial(critical, False, step),
                 [nsum_s] + sends,
                 [xg_s, xs_s],
@@ -611,14 +616,14 @@
                 [nsum_s, base_s, thin_nsum_s, ((21, 3, E), F32), ((21, 4, E), F32), ((NV * NV, E), F32)]
                 + [((41, 3, E), F32)],
                 [xs_s, xq_s],
-                [terms, d_hi, d_lo, neighbour, stiff, star, proj, lflux, own_lift, cluster, small, nflux],
+                [terms, faced, neighbour, stiff, star, proj, lflux, own_lift, cluster, small, nflux],
             )
         elif odd_step:
             nsum, base = call(
                 side,
                 [nsum_s, base_s],
                 [((3 * NBK, thin_columns), BF), ((192, thin_columns), BF)],
-                [fresh, d_hi, d_lo, neighbour, stiff, thin_star, proj, thin_lflux, own_lift, cluster]
+                [fresh, faced, neighbour, stiff, thin_star, proj, thin_lflux, own_lift, cluster]
                 + [small, came, nsum, base],
             )
         else:
@@ -626,7 +631,7 @@
                 side,
                 [nsum_s, base_s, thin_nsum_s],
                 [xs_s, xq_s],
-                [terms, d_hi, d_lo, neighbour, stiff, star, proj, lflux, own_lift, cluster, small, nsum, base],
+                [terms, faced, neighbour, stiff, star, proj, lflux, own_lift, cluster, small, nsum, base],
             )
         swapped = swapped.reshape(4, H, WIDE)
         block = jnp.concatenate([p_rest.reshape(8, H, WIDE), jnp.concatenate([swapped, swapped])], axis=1)

time: 128 us -> 127 us (level)
  Pallas kernels: 36.7 us -> 35.2 us
    pallas_call x17, Pallas kernels: 36.7 us -> 35.2 us  [call(): pl.pallas_call(kernel, out_shape=[jax.ShapeDtypeStruct(s, t) for s, t in...]
  transfers between devices with their start and end apart: 8 -> 8, of which waited for: 0 -> 4; matrix products, arithmetic and copies ran while one was open for 0% -> 0% of each run, Pallas kernels for 8% -> 7%
where the time goes in v3:
time: 127 us
  blocking collectives  89 us (70%)
  Pallas kernels  35.2 us (28%)
    all_to_all x8, blocking collectives, exchange(): lax.all_to_all(block, ('dom', 'sub'), split_axis=0, concat_axis=0, tiled=...  89 us
    pallas_call x17, Pallas kernels, call(): pl.pallas_call(kernel, out_shape=[jax.ShapeDtypeStruct(s, t) for s, t in...  35.2 us
  transfers between devices with their start and end apart: 8, of which 4 were waited for; matrix products, arithmetic and copies ran while one was open for 0% of the time, Pallas kernels for 7%

profile of v3, /device:TPU:24, one launch (start us, length us, event | category | flops | bytes accessed | tf_op | source)
XLA Modules:
  0.0 126.5 jit_solution(8228727296879239566)
XLA Ops:
  0.0 4.8 %shard_map.109 = (s32[4,128]{1,0:T(4,128)S(1)}, s32[1,128]{1,0:T(1,128)S(1)}, s32[4,128]{1,0:T(4,128)S(1)}, bf16[120,144]{1,0:T(8,128)(2,1)S(1)}, bf16[64,144]{1...) custom-call(s32[1,96]{1,0:T(1,128)} %bitcast.77, ...), custom_call_target="tpu_custom_call" | custom-call | tf_op jit(solution)/shard_map/pallas_call | solution.py:497
  4.9 1.4 %shard_map.110 = (f32[144,512]{1,0:T(8,128)S(1)}, f32[9,40,128]{2,1,0:T(8,128)S(1)}, f32[144,128]{1,0:T(8,128)S(1)}, f32[21,3,128]{2,1,0:T(4,128)S(1)}, f32[21,4...) custom-call(f32[5,9,40,128]{3,2,1,0:T(8,128)S(1)} %get-tuple-element.195.refs_0_.refs_12_.refs_13_, ...), custom_call_target="tpu_custom_call" | custom-call | tf_op jit(solution)/shard_map/pallas_call | solution.py:497
  6.3 14.8 %conditional.8 = (f32[128,144]{1,0:T(8,128)S(1)}) conditional(s32[]{:T(128)} %convert_element_type.2, f32[8,16,144]{2,1,0:T(8,128)S(1)} %maximum_maximum_fusion, (s32[]{:T(128)}, f32[8,16,144]{2,1,0:T(8,128)S(1)}) %tuple.78), branch_computations={%region_0.1_spmd, %region_1.2_spmd} | conditional | flops 27649 | bytes 294930 | solution.py:642
  6.3 14.8 %all_to_all.64 = f32[8,16,144]{2,1,0:T(8,128)S(1)} all-to-all(f32[8,16,144]{2,1,0:T(8,128)S(1)} %param), channel_id=1, replica_groups={{4,5,6,7,8,9,10,11},{12,13,14,15,16,17,18,19},{20,21,22,23,24,25,26,27}..., dimensions={0} | all-to-all | bytes 147456 | tf_op jit(solution)/shard_map/cond/branch_0_fun/all_to_all | solution.py:519
  21.2 2.6 %shard_map.111 = (f32[5,3,40,128]{3,2,1,0:T(8,128)S(1)}, bf16[288,512]{1,0:T(8,128)(2,1)S(1)}, f32[32,144]{1,0:T(8,128)S(1)}, f32[64,144]{1,0:T(8,128)S(1)}) custom-call(f32[128,144]{1,0:T(8,128)S(1)} %get-tuple-element.293.refs_0_.refs_10_, f32[144,128]{1,0:T(8,128)S(1)} %get-tuple-element.210.refs_1_, ...), custom_call_target="tpu_custom_call" | custom-call | tf_op jit(solution)/shard_map/pallas_call | solution.py:497
  25.1 10.6 %conditional.9 = (f32[128,144]{1,0:T(8,128)S(1)}) conditional(s32[]{:T(128)} %convert_element_type.2, f32[8,16,144]{2,1,0:T(8,128)S(1)} %maximum_maximum_fusion.1, (s32[]{:T(128)}, f32[8,16,144]{2,1,0:T(8,128)S(1)}) %tuple.80), branch_computations={%region_2.3_spmd, %region_3.4_spmd} | conditional | flops 27649 | bytes 294930 | solution.py:642
  25.1 10.6 %all_to_all.66 = f32[8,16,144]{2,1,0:T(8,128)S(1)} all-to-all(f32[8,16,144]{2,1,0:T(8,128)S(1)} %param.2), channel_id=1, replica_groups={{4,5,6,7,8,9,10,11},{12,13,14,15,16,17,18,19},{20,21,22,23,24,25,26,27}..., dimensions={0} | all-to-all | bytes 147456 | tf_op jit(solution)/shard_map/cond/branch_0_fun/all_to_all | solution.py:519
  35.7 2.9 %shard_map.113 = (f32[144,512]{1,0:T(8,128)S(1)}, f32[5,9,40,128]{3,2,1,0:T(8,128)S(1)}, bf16[288,512]{1,0:T(8,128)(2,1)S(1)}, f32[32,144]{1,0:T(8,128)S(1)}, f32[64,144]{1,0:T(8,128)S(1)}) custom-call(f32[128,144]{1,0:T(8,128)S(1)} %get-tuple-element.294.refs_0_, f32[144,512]{1,0:T(8,128)S(1)} %get-tuple-element.226.refs_1_, ...), custom_call_target="tpu_custom_call" | custom-call | tf_op jit(solution)/shard_map/pallas_call | solution.py:497
  38.9 1.3 shard_map.114
  40.2 10.6 %conditional.10 = (f32[128,144]{1,0:T(8,128)S(1)}) conditional(s32[]{:T(128)} %convert_element_type.2, f32[8,16,144]{2,1,0:T(8,128)S(1)} %maximum_maximum_fusion.2, (s32[]{:T(128)}, f32[8,16,144]{2,1,0:T(8,128)S(1)}) %tuple.82), branch_computations={%region_4.5_spmd, %region_5.6_spmd} | conditional | flops 27649 | bytes 294930 | solution.py:642
  40.2 10.6 %all_to_all.68 = f32[8,16,144]{2,1,0:T(8,128)S(1)} all-to-all(f32[8,16,144]{2,1,0:T(8,128)S(1)} %param.4), channel_id=1, replica_groups={{4,5,6,7,8,9,10,11},{12,13,14,15,16,17,18,19},{20,21,22,23,24,25,26,27}..., dimensions={0} | all-to-all | bytes 147456 | tf_op jit(solution)/shard_map/cond/branch_0_fun/all_to_all | solution.py:519
  50.8 2.6 %shard_map.115 = (f32[5,3,40,128]{3,2,1,0:T(8,128)S(1)}, bf16[288,512]{1,0:T(8,128)(2,1)S(1)}, f32[32,144]{1,0:T(8,128)S(1)}, f32[64,144]{1,0:T(8,128)S(1)}) custom-call(f32[128,144]{1,0:T(8,128)S(1)} %get-tuple-element.295.refs_0_.refs_10_, f32[144,128]{1,0:T(8,128)S(1)} %get-tuple-element.239.refs_1_, ...), custom_call_target="tpu_custom_call" | custom-call | tf_op jit(solution)/shard_map/pallas_call | solution.py:497
  53.5 1.0 shard_map.116
  54.7 10.6 %conditional.11 = (f32[128,144]{1,0:T(8,128)S(1)}) conditional(s32[]{:T(128)} %convert_element_type.2, f32[8,16,144]{2,1,0:T(8,128)S(1)} %maximum_maximum_fusion.3, (s32[]{:T(128)}, f32[8,16,144]{2,1,0:T(8,128)S(1)}) %tuple.84), branch_computations={%region_6.7_spmd, %region_7.8_spmd} | conditional | flops 27649 | bytes 294930 | solution.py:642
  54.8 10.6 %all_to_all.70 = f32[8,16,144]{2,1,0:T(8,128)S(1)} all-to-all(f32[8,16,144]{2,1,0:T(8,128)S(1)} %param.6), channel_id=1, replica_groups={{4,5,6,7,8,9,10,11},{12,13,14,15,16,17,18,19},{20,21,22,23,24,25,26,27}..., dimensions={0} | all-to-all | bytes 147456 | tf_op jit(solution)/shard_map/cond/branch_0_fun/all_to_all | solution.py:519
  65.4 3.4 %shard_map.117 = (f32[144,512]{1,0:T(8,128)S(1)}, f32[5,9,40,128]{3,2,1,0:T(8,128)S(1)}, bf16[288,512]{1,0:T(8,128)(2,1)S(1)}, f32[32,144]{1,0:T(8,128)S(1)}, f32[64,144]{1,0:T(8,128)S(1)}) custom-call(f32[128,144]{1,0:T(8,128)S(1)} %get-tuple-element.296.refs_0_, f32[144,512]{1,0:T(8,128)S(1)} %get-tuple-element.249.refs_1_, ...), custom_call_target="tpu_custom_call" | custom-call | tf_op jit(solution)/shard_map/pallas_call | solution.py:497
  68.9 1.3 %shard_map.118 = (f32[144,512]{1,0:T(8,128)S(1)}, f32[9,40,128]{2,1,0:T(8,128)S(1)}, f32[144,128]{1,0:T(8,128)S(1)}) custom-call(f32[5,9,40,128]{3,2,1,0:T(8,128)S(1)} %get-tuple-element.253.refs_0_.refs_12_.refs_13_, bf16[288,512]{1,0:T(8,128)(2,1)S(1)} %get-tuple-element.254.refs_1_, s32[4,128]{1,0:T(4,128)S(1)} %get-tuple-element.197.refs_2_, ...), custom_call_target="tpu_custom_call" | custom-call | tf_op jit(solution)/shard_map/pallas_call | solution.py:497
  70.2 10.6 %conditional.12 = (f32[128,144]{1,0:T(8,128)S(1)}) conditional(s32[]{:T(128)} %convert_element_type.2, f32[8,16,144]{2,1,0:T(8,128)S(1)} %maximum_maximum_fusion.4, (s32[]{:T(128)}, f32[8,16,144]{2,1,0:T(8,128)S(1)}) %tuple.86), branch_computations={%region_8.9_spmd, %region_9.10_spmd} | conditional | flops 27649 | bytes 294930 | solution.py:642
  70.2 10.6 %all_to_all.72 = f32[8,16,144]{2,1,0:T(8,128)S(1)} all-to-all(f32[8,16,144]{2,1,0:T(8,128)S(1)} %param.8), channel_id=1, replica_groups={{4,5,6,7,8,9,10,11},{12,13,14,15,16,17,18,19},{20,21,22,23,24,25,26,27}..., dimensions={0} | all-to-all | bytes 147456 | tf_op jit(solution)/shard_map/cond/branch_0_fun/all_to_all | solution.py:519
  80.8 2.6 %shard_map.119 = (f32[5,3,40,128]{3,2,1,0:T(8,128)S(1)}, bf16[288,512]{1,0:T(8,128)(2,1)S(1)}, f32[32,144]{1,0:T(8,128)S(1)}, f32[64,144]{1,0:T(8,128)S(1)}) custom-call(f32[128,144]{1,0:T(8,128)S(1)} %get-tuple-element.297.refs_0_.refs_10_, f32[144,128]{1,0:T(8,128)S(1)} %get-tuple-element.260.refs_1_, ...), custom_call_target="tpu_custom_call" | custom-call | tf_op jit(solution)/shard_map/pallas_call | solution.py:497
  83.8 1.0 shard_map.120
  85.0 10.6 %conditional.13 = (f32[128,144]{1,0:T(8,128)S(1)}) conditional(s32[]{:T(128)} %convert_element_type.2, f32[8,16,144]{2,1,0:T(8,128)S(1)} %maximum_maximum_fusion.5, (s32[]{:T(128)}, f32[8,16,144]{2,1,0:T(8,128)S(1)}) %tuple.88), branch_computations={%region_10.11_spmd, %region_11.12_spmd} | conditional | flops 27649 | bytes 294930 | solution.py:642
  85.0 10.6 %all_to_all.74 = f32[8,16,144]{2,1,0:T(8,128)S(1)} all-to-all(f32[8,16,144]{2,1,0:T(8,128)S(1)} %param.10), channel_id=1, replica_groups={{4,5,6,7,8,9,10,11},{12,13,14,15,16,17,18,19},{20,21,22,23,24,25,26,27}..., dimensions={0} | all-to-all | bytes 147456 | tf_op jit(solution)/shard_map/cond/branch_0_fun/all_to_all | solution.py:519
  95.6 2.9 %shard_map.121 = (f32[144,512]{1,0:T(8,128)S(1)}, f32[5,9,40,128]{3,2,1,0:T(8,128)S(1)}, bf16[288,512]{1,0:T(8,128)(2,1)S(1)}, f32[32,144]{1,0:T(8,128)S(1)}, f32[64,144]{1,0:T(8,128)S(1)}) custom-call(f32[128,144]{1,0:T(8,128)S(1)} %get-tuple-element.298.refs_0_, f32[144,512]{1,0:T(8,128)S(1)} %get-tuple-element.270.refs_1_, ...), custom_call_target="tpu_custom_call" | custom-call | tf_op jit(solution)/shard_map/pallas_call | solution.py:497
  98.6 1.3 shard_map.122
  99.9 10.6 %conditional.14 = (f32[128,144]{1,0:T(8,128)S(1)}) conditional(s32[]{:T(128)} %convert_element_type.2, f32[8,16,144]{2,1,0:T(8,128)S(1)} %maximum_maximum_fusion.6, (s32[]{:T(128)}, f32[8,16,144]{2,1,0:T(8,128)S(1)}) %tuple.90), branch_computations={%region_12.13_spmd, %region_13.14_spmd} | conditional | flops 27649 | bytes 294930 | solution.py:642
  100.0 10.6 %all_to_all.76 = f32[8,16,144]{2,1,0:T(8,128)S(1)} all-to-all(f32[8,16,144]{2,1,0:T(8,128)S(1)} %param.12), channel_id=1, replica_groups={{4,5,6,7,8,9,10,11},{12,13,14,15,16,17,18,19},{20,21,22,23,24,25,26,27}..., dimensions={0} | all-to-all | bytes 147456 | tf_op jit(solution)/shard_map/cond/branch_0_fun/all_to_all | solution.py:519
  110.5 2.6 %shard_map.123 = (f32[5,3,40,128]{3,2,1,0:T(8,128)S(1)}, bf16[288,512]{1,0:T(8,128)(2,1)S(1)}, f32[32,144]{1,0:T(8,128)S(1)}, f32[64,144]{1,0:T(8,128)S(1)}) custom-call(f32[128,144]{1,0:T(8,128)S(1)} %get-tuple-element.299.refs_0_.refs_10_, f32[144,128]{1,0:T(8,128)S(1)} %get-tuple-element.281.refs_1_, ...), custom_call_target="tpu_custom_call" | custom-call | tf_op jit(solution)/shard_map/pallas_call | solution.py:497
  113.2 1.0 shard_map.124
  114.5 10.6 %conditional.15 = (f32[128,144]{1,0:T(8,128)S(1)}) conditional(s32[]{:T(128)} %convert_element_type.2, f32[8,16,144]{2,1,0:T(8,128)S(1)} %maximum_maximum_fusion.7, (s32[]{:T(128)}, f32[8,16,144]{2,1,0:T(8,128)S(1)}) %tuple.92), branch_computations={%region_14.15_spmd, %region_15.16_spmd} | conditional | flops 27649 | bytes 294930 | solution.py:642
  114.5 10.6 %all_to_all.78 = f32[8,16,144]{2,1,0:T(8,128)S(1)} all-to-all(f32[8,16,144]{2,1,0:T(8,128)S(1)} %param.14), channel_id=1, replica_groups={{4,5,6,7,8,9,10,11},{12,13,14,15,16,17,18,19},{20,21,22,23,24,25,26,27}..., dimensions={0} | all-to-all | bytes 147456 | tf_op jit(solution)/shard_map/cond/branch_0_fun/all_to_all | solution.py:519
  125.1 1.5 %shard_map.125 = f32[9,35,128]{2,1,0:T(8,128)} custom-call(f32[128,144]{1,0:T(8,128)S(1)} %get-tuple-element.300.refs_0_, f32[144,512]{1,0:T(8,128)S(1)} %get-tuple-element.291.refs_1_, f32[9,40,128]{2,1,0:T(8,128)S(1)} %get-tuple-element.292.refs_2_, f32[9,9,4,128]{3,2,1,0:T(4,128)S(1)} %get-tuple-element.205.refs_10_.refs_3_, ...), custom_call_target="tpu_custom_call" | custom-call | tf_op jit(solution)/shard_map/pallas_call | solution.py:497
  (26 shorter events, 3.0 us)
Async XLA Ops:
  4.8 1.5 %collective-permute-start = (f32[32,144]{1,0:T(8,128)S(1)}, f32[32,144]{1,0:T(8,128)S(1)}, u32[]{:S(2)}, u32[]{:S(2)}) collective-permute-start(f32[32,144]{1,0:T(8,128)S(1)} %get-tuple-element.194), channel_id=1, source_target_pairs={{0,4},{4,0},{8,12},{12,8},{16,20},{20,16},{24,28},{28,24},{32,36},... | collective-permute-start | bytes 55304 | tf_op jit(solution)/shard_map/ppermute | solution.py:610
  23.8 1.3 %collective-permute-start.1 = (f32[32,144]{1,0:T(8,128)S(1)}, f32[32,144]{1,0:T(8,128)S(1)}, u32[]{:S(2)}, u32[]{:S(2)}) collective-permute-start(f32[32,144]{1,0:T(8,128)S(1)} %get-tuple-element.218), channel_id=1, source_target_pairs={{0,4},{4,0},{8,12},{12,8},{16,20},{20,16},{24,28},{28,24},{32,36},... | collective-permute-start | bytes 55304 | tf_op jit(solution)/shard_map/ppermute | solution.py:610
  38.6 1.6 %collective-permute-start.2 = (f32[32,144]{1,0:T(8,128)S(1)}, f32[32,144]{1,0:T(8,128)S(1)}, u32[]{:S(2)}, u32[]{:S(2)}) collective-permute-start(f32[32,144]{1,0:T(8,128)S(1)} %get-tuple-element.231), channel_id=1, source_target_pairs={{0,4},{4,0},{8,12},{12,8},{16,20},{20,16},{24,28},{28,24},{32,36},... | collective-permute-start | bytes 55304 | tf_op jit(solution)/shard_map/ppermute | solution.py:610
  53.4 1.3 %collective-permute-start.3 = (f32[32,144]{1,0:T(8,128)S(1)}, f32[32,144]{1,0:T(8,128)S(1)}, u32[]{:S(2)}, u32[]{:S(2)}) collective-permute-start(f32[32,144]{1,0:T(8,128)S(1)} %get-tuple-element.242), channel_id=1, source_target_pairs={{0,4},{4,0},{8,12},{12,8},{16,20},{20,16},{24,28},{28,24},{32,36},... | collective-permute-start | bytes 55304 | tf_op jit(solution)/shard_map/ppermute | solution.py:610
  68.8 1.4 %collective-permute-start.4 = (f32[32,144]{1,0:T(8,128)S(1)}, f32[32,144]{1,0:T(8,128)S(1)}, u32[]{:S(2)}, u32[]{:S(2)}) collective-permute-start(f32[32,144]{1,0:T(8,128)S(1)} %get-tuple-element.252), channel_id=1, source_target_pairs={{0,4},{4,0},{8,12},{12,8},{16,20},{20,16},{24,28},{28,24},{32,36},... | collective-permute-start | bytes 55304 | tf_op jit(solution)/shard_map/ppermute | solution.py:610
  83.5 1.5 %collective-permute-start.5 = (f32[32,144]{1,0:T(8,128)S(1)}, f32[32,144]{1,0:T(8,128)S(1)}, u32[]{:S(2)}, u32[]{:S(2)}) collective-permute-start(f32[32,144]{1,0:T(8,128)S(1)} %get-tuple-element.263), channel_id=1, source_target_pairs={{0,4},{4,0},{8,12},{12,8},{16,20},{20,16},{24,28},{28,24},{32,36},... | collective-permute-start | bytes 55304 | tf_op jit(solution)/shard_map/ppermute | solution.py:610
  98.5 1.4 %collective-permute-start.6 = (f32[32,144]{1,0:T(8,128)S(1)}, f32[32,144]{1,0:T(8,128)S(1)}, u32[]{:S(2)}, u32[]{:S(2)}) collective-permute-start(f32[32,144]{1,0:T(8,128)S(1)} %get-tuple-element.273), channel_id=1, source_target_pairs={{0,4},{4,0},{8,12},{12,8},{16,20},{20,16},{24,28},{28,24},{32,36},... | collective-permute-start | bytes 55304 | tf_op jit(solution)/shard_map/ppermute | solution.py:610
  113.1 1.3 %collective-permute-start.7 = (f32[32,144]{1,0:T(8,128)S(1)}, f32[32,144]{1,0:T(8,128)S(1)}, u32[]{:S(2)}, u32[]{:S(2)}) collective-permute-start(f32[32,144]{1,0:T(8,128)S(1)} %get-tuple-element.284), channel_id=1, source_target_pairs={{0,4},{4,0},{8,12},{12,8},{16,20},{20,16},{24,28},{28,24},{32,36},... | collective-permute-start | bytes 55304 | tf_op jit(solution)/shard_map/ppermute | solution.py:610

commit v4 on v3

--- a/solution.py
+++ b/solution.py
@@ -443,6 +443,8 @@
     held = [[terms[k, v] for v in range(wide)] for k in range(ORDER)]
     if thin:
         final = derive_thin(held[ORDER - 1], stiff, star, xs)
+    elif step % 4 == 2:
+        final = apart(derive_thin(side_by_side(held[ORDER - 1], 2), stiff, star, xs, 2), 2)
     else:
         final = derive(held[ORDER - 1], stiff, star, xs)
     state = []
@@ -631,7 +633,8 @@
                 side,
                 [nsum_s, base_s, thin_nsum_s],
                 [xs_s, xq_s],
-                [terms, faced, neighbour, stiff, star, proj, lflux, own_lift, cluster, small, nsum, base],
+                [terms, faced, neighbour, stiff, pair_star if step % 4 == 2 else star, proj, lflux, own_lift, cluster]
+                + [small, nsum, base],
             )
         swapped = swapped.reshape(4, H, WIDE)
         block = jnp.concatenate([p_rest.reshape(8, H, WIDE), jnp.concatenate([swapped, swapped])], axis=1)

time: 127 us -> 127 us (level)
  transfers between devices with their start and end apart: 8 -> 8, of which waited for: 4 -> 6; matrix products, arithmetic and copies ran while one was open for 0% -> 0% of each run, Pallas kernels for 7% -> 7%
where the time goes in v4:
time: 127 us; the launch traced here: 126 us
  blocking collectives  89 us (70%)
  Pallas kernels  34.9 us (27%)
    all_to_all x8, blocking collectives, exchange(): lax.all_to_all(block, ('dom', 'sub'), split_axis=0, concat_axis=0, tiled=...  89 us
    pallas_call x17, Pallas kernels, call(): pl.pallas_call(kernel, out_shape=[jax.ShapeDtypeStruct(s, t) for s, t in...  34.9 us
  transfers between devices with their start and end apart: 8, of which 6 were waited for; matrix products, arithmetic and copies ran while one was open for 0% of the time, Pallas kernels for 7%

profile of v4, /device:TPU:24, one launch (start us, length us, event | category | flops | bytes accessed | tf_op | source)
XLA Modules:
  0.0 126.4 jit_solution(11242118144698172855)
XLA Ops:
  0.0 4.8 %shard_map.109 = (s32[4,128]{1,0:T(4,128)S(1)}, s32[1,128]{1,0:T(1,128)S(1)}, s32[4,128]{1,0:T(4,128)S(1)}, bf16[120,144]{1,0:T(8,128)(2,1)S(1)}, bf16[64,144]{1...) custom-call(s32[1,96]{1,0:T(1,128)} %bitcast.77, ...), custom_call_target="tpu_custom_call" | custom-call | tf_op jit(solution)/shard_map/pallas_call | solution.py:499
  4.9 1.4 %shard_map.110 = (f32[144,512]{1,0:T(8,128)S(1)}, f32[9,40,128]{2,1,0:T(8,128)S(1)}, f32[144,128]{1,0:T(8,128)S(1)}, f32[21,3,128]{2,1,0:T(4,128)S(1)}, f32[21,4...) custom-call(f32[5,9,40,128]{3,2,1,0:T(8,128)S(1)} %get-tuple-element.195.refs_0_.refs_12_.refs_13_, ...), custom_call_target="tpu_custom_call" | custom-call | tf_op jit(solution)/shard_map/pallas_call | solution.py:499
  6.3 14.8 %conditional.8 = (f32[128,144]{1,0:T(8,128)S(1)}) conditional(s32[]{:T(128)} %convert_element_type.2, f32[8,16,144]{2,1,0:T(8,128)S(1)} %maximum_maximum_fusion, (s32[]{:T(128)}, f32[8,16,144]{2,1,0:T(8,128)S(1)}) %tuple.78), branch_computations={%region_0.1_spmd, %region_1.2_spmd} | conditional | flops 27649 | bytes 294930 | solution.py:645
  6.3 14.8 %all_to_all.64 = f32[8,16,144]{2,1,0:T(8,128)S(1)} all-to-all(f32[8,16,144]{2,1,0:T(8,128)S(1)} %param), channel_id=1, replica_groups={{4,5,6,7,8,9,10,11},{12,13,14,15,16,17,18,19},{20,21,22,23,24,25,26,27}..., dimensions={0} | all-to-all | bytes 147456 | tf_op jit(solution)/shard_map/cond/branch_0_fun/all_to_all | solution.py:521
  21.2 2.6 %shard_map.111 = (f32[5,3,40,128]{3,2,1,0:T(8,128)S(1)}, bf16[288,512]{1,0:T(8,128)(2,1)S(1)}, f32[32,144]{1,0:T(8,128)S(1)}, f32[64,144]{1,0:T(8,128)S(1)}) custom-call(f32[128,144]{1,0:T(8,128)S(1)} %get-tuple-element.293.refs_0_.refs_10_, f32[144,128]{1,0:T(8,128)S(1)} %get-tuple-element.210.refs_1_, ...), custom_call_target="tpu_custom_call" | custom-call | tf_op jit(solution)/shard_map/pallas_call | solution.py:499
  25.1 10.6 %conditional.9 = (f32[128,144]{1,0:T(8,128)S(1)}) conditional(s32[]{:T(128)} %convert_element_type.2, f32[8,16,144]{2,1,0:T(8,128)S(1)} %maximum_maximum_fusion.1, (s32[]{:T(128)}, f32[8,16,144]{2,1,0:T(8,128)S(1)}) %tuple.80), branch_computations={%region_2.3_spmd, %region_3.4_spmd} | conditional | flops 27649 | bytes 294930 | solution.py:645
  25.1 10.6 %all_to_all.66 = f32[8,16,144]{2,1,0:T(8,128)S(1)} all-to-all(f32[8,16,144]{2,1,0:T(8,128)S(1)} %param.2), channel_id=1, replica_groups={{4,5,6,7,8,9,10,11},{12,13,14,15,16,17,18,19},{20,21,22,23,24,25,26,27}..., dimensions={0} | all-to-all | bytes 147456 | tf_op jit(solution)/shard_map/cond/branch_0_fun/all_to_all | solution.py:521
  35.7 3.0 %shard_map.113 = (f32[144,512]{1,0:T(8,128)S(1)}, f32[5,9,40,128]{3,2,1,0:T(8,128)S(1)}, bf16[288,512]{1,0:T(8,128)(2,1)S(1)}, f32[32,144]{1,0:T(8,128)S(1)}, f32[64,144]{1,0:T(8,128)S(1)}) custom-call(f32[128,144]{1,0:T(8,128)S(1)} %get-tuple-element.294.refs_0_, f32[144,512]{1,0:T(8,128)S(1)} %get-tuple-element.226.refs_1_, ...), custom_call_target="tpu_custom_call" | custom-call | tf_op jit(solution)/shard_map/pallas_call | solution.py:499
  39.0 1.1 shard_map.114
  40.2 10.6 %conditional.10 = (f32[128,144]{1,0:T(8,128)S(1)}) conditional(s32[]{:T(128)} %convert_element_type.2, f32[8,16,144]{2,1,0:T(8,128)S(1)} %maximum_maximum_fusion.2, (s32[]{:T(128)}, f32[8,16,144]{2,1,0:T(8,128)S(1)}) %tuple.82), branch_computations={%region_4.5_spmd, %region_5.6_spmd} | conditional | flops 27649 | bytes 294930 | solution.py:645
  40.2 10.6 %all_to_all.68 = f32[8,16,144]{2,1,0:T(8,128)S(1)} all-to-all(f32[8,16,144]{2,1,0:T(8,128)S(1)} %param.4), channel_id=1, replica_groups={{4,5,6,7,8,9,10,11},{12,13,14,15,16,17,18,19},{20,21,22,23,24,25,26,27}..., dimensions={0} | all-to-all | bytes 147456 | tf_op jit(solution)/shard_map/cond/branch_0_fun/all_to_all | solution.py:521
  50.8 2.6 %shard_map.115 = (f32[5,3,40,128]{3,2,1,0:T(8,128)S(1)}, bf16[288,512]{1,0:T(8,128)(2,1)S(1)}, f32[32,144]{1,0:T(8,128)S(1)}, f32[64,144]{1,0:T(8,128)S(1)}) custom-call(f32[128,144]{1,0:T(8,128)S(1)} %get-tuple-element.295.refs_0_.refs_10_, f32[144,128]{1,0:T(8,128)S(1)} %get-tuple-element.239.refs_1_, ...), custom_call_target="tpu_custom_call" | custom-call | tf_op jit(solution)/shard_map/pallas_call | solution.py:499
  53.5 1.0 shard_map.116
  54.7 10.6 %conditional.11 = (f32[128,144]{1,0:T(8,128)S(1)}) conditional(s32[]{:T(128)} %convert_element_type.2, f32[8,16,144]{2,1,0:T(8,128)S(1)} %maximum_maximum_fusion.3, (s32[]{:T(128)}, f32[8,16,144]{2,1,0:T(8,128)S(1)}) %tuple.84), branch_computations={%region_6.7_spmd, %region_7.8_spmd} | conditional | flops 27649 | bytes 294930 | solution.py:645
  54.7 10.6 %all_to_all.70 = f32[8,16,144]{2,1,0:T(8,128)S(1)} all-to-all(f32[8,16,144]{2,1,0:T(8,128)S(1)} %param.6), channel_id=1, replica_groups={{4,5,6,7,8,9,10,11},{12,13,14,15,16,17,18,19},{20,21,22,23,24,25,26,27}..., dimensions={0} | all-to-all | bytes 147456 | tf_op jit(solution)/shard_map/cond/branch_0_fun/all_to_all | solution.py:521
  65.3 3.4 %shard_map.117 = (f32[144,512]{1,0:T(8,128)S(1)}, f32[5,9,40,128]{3,2,1,0:T(8,128)S(1)}, bf16[288,512]{1,0:T(8,128)(2,1)S(1)}, f32[32,144]{1,0:T(8,128)S(1)}, f32[64,144]{1,0:T(8,128)S(1)}) custom-call(f32[128,144]{1,0:T(8,128)S(1)} %get-tuple-element.296.refs_0_, f32[144,512]{1,0:T(8,128)S(1)} %get-tuple-element.249.refs_1_, ...), custom_call_target="tpu_custom_call" | custom-call | tf_op jit(solution)/shard_map/pallas_call | solution.py:499
  68.8 1.3 %shard_map.118 = (f32[144,512]{1,0:T(8,128)S(1)}, f32[9,40,128]{2,1,0:T(8,128)S(1)}, f32[144,128]{1,0:T(8,128)S(1)}) custom-call(f32[5,9,40,128]{3,2,1,0:T(8,128)S(1)} %get-tuple-element.253.refs_0_.refs_12_.refs_13_, bf16[288,512]{1,0:T(8,128)(2,1)S(1)} %get-tuple-element.254.refs_1_, s32[4,128]{1,0:T(4,128)S(1)} %get-tuple-element.197.refs_2_, ...), custom_call_target="tpu_custom_call" | custom-call | tf_op jit(solution)/shard_map/pallas_call | solution.py:499
  70.2 10.6 %conditional.12 = (f32[128,144]{1,0:T(8,128)S(1)}) conditional(s32[]{:T(128)} %convert_element_type.2, f32[8,16,144]{2,1,0:T(8,128)S(1)} %maximum_maximum_fusion.4, (s32[]{:T(128)}, f32[8,16,144]{2,1,0:T(8,128)S(1)}) %tuple.86), branch_computations={%region_8.9_spmd, %region_9.10_spmd} | conditional | flops 27649 | bytes 294930 | solution.py:645
  70.2 10.6 %all_to_all.72 = f32[8,16,144]{2,1,0:T(8,128)S(1)} all-to-all(f32[8,16,144]{2,1,0:T(8,128)S(1)} %param.8), channel_id=1, replica_groups={{4,5,6,7,8,9,10,11},{12,13,14,15,16,17,18,19},{20,21,22,23,24,25,26,27}..., dimensions={0} | all-to-all | bytes 147456 | tf_op jit(solution)/shard_map/cond/branch_0_fun/all_to_all | solution.py:521
  80.8 2.6 %shard_map.119 = (f32[5,3,40,128]{3,2,1,0:T(8,128)S(1)}, bf16[288,512]{1,0:T(8,128)(2,1)S(1)}, f32[32,144]{1,0:T(8,128)S(1)}, f32[64,144]{1,0:T(8,128)S(1)}) custom-call(f32[128,144]{1,0:T(8,128)S(1)} %get-tuple-element.297.refs_0_.refs_10_, f32[144,128]{1,0:T(8,128)S(1)} %get-tuple-element.260.refs_1_, ...), custom_call_target="tpu_custom_call" | custom-call | tf_op jit(solution)/shard_map/pallas_call | solution.py:499
  83.7 1.0 shard_map.120
  84.9 10.6 %conditional.13 = (f32[128,144]{1,0:T(8,128)S(1)}) conditional(s32[]{:T(128)} %convert_element_type.2, f32[8,16,144]{2,1,0:T(8,128)S(1)} %maximum_maximum_fusion.5, (s32[]{:T(128)}, f32[8,16,144]{2,1,0:T(8,128)S(1)}) %tuple.88), branch_computations={%region_10.11_spmd, %region_11.12_spmd} | conditional | flops 27649 | bytes 294930 | solution.py:645
  85.0 10.6 %all_to_all.74 = f32[8,16,144]{2,1,0:T(8,128)S(1)} all-to-all(f32[8,16,144]{2,1,0:T(8,128)S(1)} %param.10), channel_id=1, replica_groups={{4,5,6,7,8,9,10,11},{12,13,14,15,16,17,18,19},{20,21,22,23,24,25,26,27}..., dimensions={0} | all-to-all | bytes 147456 | tf_op jit(solution)/shard_map/cond/branch_0_fun/all_to_all | solution.py:521
  95.5 3.0 %shard_map.121 = (f32[144,512]{1,0:T(8,128)S(1)}, f32[5,9,40,128]{3,2,1,0:T(8,128)S(1)}, bf16[288,512]{1,0:T(8,128)(2,1)S(1)}, f32[32,144]{1,0:T(8,128)S(1)}, f32[64,144]{1,0:T(8,128)S(1)}) custom-call(f32[128,144]{1,0:T(8,128)S(1)} %get-tuple-element.298.refs_0_, f32[144,512]{1,0:T(8,128)S(1)} %get-tuple-element.270.refs_1_, ...), custom_call_target="tpu_custom_call" | custom-call | tf_op jit(solution)/shard_map/pallas_call | solution.py:499
  98.6 1.1 shard_map.122
  99.8 10.6 %conditional.14 = (f32[128,144]{1,0:T(8,128)S(1)}) conditional(s32[]{:T(128)} %convert_element_type.2, f32[8,16,144]{2,1,0:T(8,128)S(1)} %maximum_maximum_fusion.6, (s32[]{:T(128)}, f32[8,16,144]{2,1,0:T(8,128)S(1)}) %tuple.90), branch_computations={%region_12.13_spmd, %region_13.14_spmd} | conditional | flops 27649 | bytes 294930 | solution.py:645
  99.8 10.6 %all_to_all.76 = f32[8,16,144]{2,1,0:T(8,128)S(1)} all-to-all(f32[8,16,144]{2,1,0:T(8,128)S(1)} %param.12), channel_id=1, replica_groups={{4,5,6,7,8,9,10,11},{12,13,14,15,16,17,18,19},{20,21,22,23,24,25,26,27}..., dimensions={0} | all-to-all | bytes 147456 | tf_op jit(solution)/shard_map/cond/branch_0_fun/all_to_all | solution.py:521
  110.4 2.6 %shard_map.123 = (f32[5,3,40,128]{3,2,1,0:T(8,128)S(1)}, bf16[288,512]{1,0:T(8,128)(2,1)S(1)}, f32[32,144]{1,0:T(8,128)S(1)}, f32[64,144]{1,0:T(8,128)S(1)}) custom-call(f32[128,144]{1,0:T(8,128)S(1)} %get-tuple-element.299.refs_0_.refs_10_, f32[144,128]{1,0:T(8,128)S(1)} %get-tuple-element.281.refs_1_, ...), custom_call_target="tpu_custom_call" | custom-call | tf_op jit(solution)/shard_map/pallas_call | solution.py:499
  113.2 1.0 shard_map.124
  114.4 10.6 %conditional.15 = (f32[128,144]{1,0:T(8,128)S(1)}) conditional(s32[]{:T(128)} %convert_element_type.2, f32[8,16,144]{2,1,0:T(8,128)S(1)} %maximum_maximum_fusion.7, (s32[]{:T(128)}, f32[8,16,144]{2,1,0:T(8,128)S(1)}) %tuple.92), branch_computations={%region_14.15_spmd, %region_15.16_spmd} | conditional | flops 27649 | bytes 294930 | solution.py:645
  114.4 10.6 %all_to_all.78 = f32[8,16,144]{2,1,0:T(8,128)S(1)} all-to-all(f32[8,16,144]{2,1,0:T(8,128)S(1)} %param.14), channel_id=1, replica_groups={{4,5,6,7,8,9,10,11},{12,13,14,15,16,17,18,19},{20,21,22,23,24,25,26,27}..., dimensions={0} | all-to-all | bytes 147456 | tf_op jit(solution)/shard_map/cond/branch_0_fun/all_to_all | solution.py:521
  125.0 1.5 %shard_map.125 = f32[9,35,128]{2,1,0:T(8,128)} custom-call(f32[128,144]{1,0:T(8,128)S(1)} %get-tuple-element.300.refs_0_, f32[144,512]{1,0:T(8,128)S(1)} %get-tuple-element.291.refs_1_, f32[9,40,128]{2,1,0:T(8,128)S(1)} %get-tuple-element.292.refs_2_, f32[9,9,4,128]{3,2,1,0:T(4,128)S(1)} %get-tuple-element.205.refs_10_.refs_3_, ...), custom_call_target="tpu_custom_call" | custom-call | tf_op jit(solution)/shard_map/pallas_call | solution.py:499
  (26 shorter events, 3.2 us)
Async XLA Ops:
  4.8 1.5 %collective-permute-start = (f32[32,144]{1,0:T(8,128)S(1)}, f32[32,144]{1,0:T(8,128)S(1)}, u32[]{:S(2)}, u32[]{:S(2)}) collective-permute-start(f32[32,144]{1,0:T(8,128)S(1)} %get-tuple-element.194), channel_id=1, source_target_pairs={{0,4},{4,0},{8,12},{12,8},{16,20},{20,16},{24,28},{28,24},{32,36},... | collective-permute-start | bytes 55304 | tf_op jit(solution)/shard_map/ppermute | solution.py:612
  23.8 1.3 %collective-permute-start.1 = (f32[32,144]{1,0:T(8,128)S(1)}, f32[32,144]{1,0:T(8,128)S(1)}, u32[]{:S(2)}, u32[]{:S(2)}) collective-permute-start(f32[32,144]{1,0:T(8,128)S(1)} %get-tuple-element.218), channel_id=1, source_target_pairs={{0,4},{4,0},{8,12},{12,8},{16,20},{20,16},{24,28},{28,24},{32,36},... | collective-permute-start | bytes 55304 | tf_op jit(solution)/shard_map/ppermute | solution.py:612
  38.7 1.5 %collective-permute-start.2 = (f32[32,144]{1,0:T(8,128)S(1)}, f32[32,144]{1,0:T(8,128)S(1)}, u32[]{:S(2)}, u32[]{:S(2)}) collective-permute-start(f32[32,144]{1,0:T(8,128)S(1)} %get-tuple-element.231), channel_id=1, source_target_pairs={{0,4},{4,0},{8,12},{12,8},{16,20},{20,16},{24,28},{28,24},{32,36},... | collective-permute-start | bytes 55304 | tf_op jit(solution)/shard_map/ppermute | solution.py:612
  53.4 1.3 %collective-permute-start.3 = (f32[32,144]{1,0:T(8,128)S(1)}, f32[32,144]{1,0:T(8,128)S(1)}, u32[]{:S(2)}, u32[]{:S(2)}) collective-permute-start(f32[32,144]{1,0:T(8,128)S(1)} %get-tuple-element.242), channel_id=1, source_target_pairs={{0,4},{4,0},{8,12},{12,8},{16,20},{20,16},{24,28},{28,24},{32,36},... | collective-permute-start | bytes 55304 | tf_op jit(solution)/shard_map/ppermute | solution.py:612
  68.7 1.4 %collective-permute-start.4 = (f32[32,144]{1,0:T(8,128)S(1)}, f32[32,144]{1,0:T(8,128)S(1)}, u32[]{:S(2)}, u32[]{:S(2)}) collective-permute-start(f32[32,144]{1,0:T(8,128)S(1)} %get-tuple-element.252), channel_id=1, source_target_pairs={{0,4},{4,0},{8,12},{12,8},{16,20},{20,16},{24,28},{28,24},{32,36},... | collective-permute-start | bytes 55304 | tf_op jit(solution)/shard_map/ppermute | solution.py:612
  83.4 1.5 %collective-permute-start.5 = (f32[32,144]{1,0:T(8,128)S(1)}, f32[32,144]{1,0:T(8,128)S(1)}, u32[]{:S(2)}, u32[]{:S(2)}) collective-permute-start(f32[32,144]{1,0:T(8,128)S(1)} %get-tuple-element.263), channel_id=1, source_target_pairs={{0,4},{4,0},{8,12},{12,8},{16,20},{20,16},{24,28},{28,24},{32,36},... | collective-permute-start | bytes 55304 | tf_op jit(solution)/shard_map/ppermute | solution.py:612
  98.5 1.3 %collective-permute-start.6 = (f32[32,144]{1,0:T(8,128)S(1)}, f32[32,144]{1,0:T(8,128)S(1)}, u32[]{:S(2)}, u32[]{:S(2)}) collective-permute-start(f32[32,144]{1,0:T(8,128)S(1)} %get-tuple-element.273), channel_id=1, source_target_pairs={{0,4},{4,0},{8,12},{12,8},{16,20},{20,16},{24,28},{28,24},{32,36},... | collective-permute-start | bytes 55304 | tf_op jit(solution)/shard_map/ppermute | solution.py:612
  113.1 1.3 %collective-permute-start.7 = (f32[32,144]{1,0:T(8,128)S(1)}, f32[32,144]{1,0:T(8,128)S(1)}, u32[]{:S(2)}, u32[]{:S(2)}) collective-permute-start(f32[32,144]{1,0:T(8,128)S(1)} %get-tuple-element.284), channel_id=1, source_target_pairs={{0,4},{4,0},{8,12},{12,8},{16,20},{20,16},{24,28},{28,24},{32,36},... | collective-permute-start | bytes 55304 | tf_op jit(solution)/shard_map/ppermute | solution.py:612
